TPU v7x, 256 devices: a whole 4x4x8 slice. The times are simulated.
256 devices in a mesh: ctx: 8 (over y, core), exp: 32 (over z, x).
Axes of the slice: x: 4, y: 4, z: 8, core: 2. Of those that a mesh axis runs over, the one named last changes fastest.
Arguments:
- tokens: bfloat16 [32, 1024, 2560], P('exp', 'ctx'), may hold values from -6 to 6
- router: bfloat16 [2560, 64], replicated, may hold values from -0.125 to 0.125
- expert_gate_up: bfloat16 [64, 2560, 512], P('exp', 'ctx'), may hold values from -0.125 to 0.125
- expert_down: bfloat16 [64, 256, 2560], P('exp', 'ctx'), may hold values from -0.375 to 0.375
- shared_gate_up: bfloat16 [2560, 512], replicated, may hold values from -0.125 to 0.125
- shared_down: bfloat16 [256, 2560], replicated, may hold values from -0.375 to 0.375
- expert_index_table: int32 [32, 1024, 8], P('exp', 'ctx'), may hold values from 0 to 63, all different within a row; in each aligned block of 128 rows (0 to 127, 128 to 255, ..., all dimensions but the last counted through in order) at most 20 rows name the same one
- document_length_table: int32 [32, 8], P('exp'), may hold values from 1 to 512, 1024 in all within a row
- step_sizes_unsoftened: float32 [32, 1024, 40], P('exp', 'ctx'), may hold values from -4 to 4
- state_input_vectors: bfloat16 [32, 1024, 128], P('exp', 'ctx'), may hold values from -0.8984375 to 0.8984375
- state_output_vectors: bfloat16 [32, 1024, 128], P('exp', 'ctx'), may hold values from -0.5 to 0.5
- decay_rate: float32 [40], replicated, may hold values from 0.00048828125 to 0.05
- skip_gain: float32 [40], replicated, may hold values from 0.25 to 1
- cotangent: bfloat16 [32, 1024, 2560], P('exp', 'ctx'), may hold values from -6 to 6
Outputs:
- mixed: bfloat16 [32, 1024, 2560], P('exp', 'ctx')
- input_grad: bfloat16 [32, 1024, 2560], P('exp', 'ctx')
Inputs may be any that keep to these rules, and one draw needn't show every extreme that they name: `expert_index_table`: in each aligned block of 128 positions (those of one device) each position names 8 different experts and no expert is named more than 20 times; some expert is named exactly 20 times. `document_length_table`: each row's lengths sum to 1024.
All inputs are finite; a program needn't handle non-finite values.
Results may differ from a plain program's by a relative error of at most 0.008.
Values may be sent and summed in bfloat16 or wider, within the bound.
A program may use at most 128 MiB of HBM per device.

v0:
```python
import jax
import jax.numpy as jnp
from jax import lax
from jax.sharding import PartitionSpec as P

highest = lax.Precision.HIGHEST


def carried_in(part, axis, combine, identity, reverse):
    count = lax.axis_size(axis)
    place = lax.axis_index(axis)
    ahead = count - 1 - place if reverse else place
    gathered = jax.tree.map(lambda a: lax.all_gather(a, axis), part)
    state = jax.tree.map(lambda a, e: jnp.zeros_like(a) + jnp.asarray(e, a.dtype), part, identity)

    def one(turn, state):
        source = count - 1 - turn if reverse else turn
        return combine(
            state, jax.tree.map(lambda a: lax.dynamic_index_in_dim(a, source, 0, False), gathered)
        )

    return lax.fori_loop(0, ahead, one, state)


def document_index(starts, positions):
    return jnp.sum((starts[None, :] <= positions[:, None]).astype(jnp.int32), axis=1) - 1


def state_block(carry_state, block_inputs, decay_rate):
    values, step_sizes, write_half, read_half, documents, before = block_inputs
    writes = write_half.astype(jnp.float32)
    read_vectors = read_half.astype(jnp.float32)
    cumulative = jnp.cumsum(-step_sizes * decay_rate[None, :], axis=0)
    token_order = jnp.arange(documents.shape[0], dtype=jnp.int32)
    causal = (documents[:, None] == documents[None, :]) & (
        token_order[:, None] >= token_order[None, :]
    )
    spread = cumulative.T[:, :, None] - cumulative.T[:, None, :]
    decayed = jnp.where(causal[None], jnp.exp(jnp.where(causal[None], spread, 0.0)), 0.0)
    affinity = jnp.einsum("tn,sn->ts", read_half, write_half, preferred_element_type=jnp.float32)
    weights = affinity[None] * decayed * step_sizes.T[:, None, :]
    output = jnp.einsum("hts,shp->thp", weights, values, precision=highest)
    carried = jnp.exp(cumulative) * (documents == before).astype(jnp.float32)[:, None]
    output = output + carried[:, :, None] * jnp.einsum(
        "hpn,tn->thp", carry_state, read_vectors, precision=highest
    )
    closing = (
        jnp.exp(cumulative[-1][None, :] - cumulative)
        * (documents == documents[-1]).astype(jnp.float32)[:, None]
        * step_sizes
    )
    keep_factor = jnp.exp(cumulative[-1]) * (documents[-1] == before).astype(jnp.float32)
    carry_state = keep_factor[:, None, None] * carry_state + jnp.einsum(
        "sh,shp,sn->hpn", closing, values, writes, precision=highest
    )
    return (carry_state, (output, weights, carried, closing, keep_factor))


def combine_states(earlier, later):
    return (earlier[0] * later[0], later[0][:, None, None] * earlier[1] + later[1])


def on_device(
    tokens,
    router,
    expert_gate_up,
    expert_down,
    shared_gate_up,
    shared_down,
    expert_index_table,
    document_length_table,
    step_sizes_unsoftened,
    state_input_vectors,
    state_output_vectors,
    decay_rate,
    skip_gain,
    cotangent,
):
    features = tokens[0]
    length = features.shape[0]
    model_width = features.shape[1]
    groups = lax.axis_size("exp")
    local_count = expert_gate_up.shape[0]
    expert_total = router.shape[1]
    top_count = expert_index_table.shape[2]
    capacity = 5 * length * top_count // (4 * expert_total)
    hidden_units = expert_gate_up.shape[2] // 2
    routes = expert_index_table[0]
    logits = jnp.dot(features, router, preferred_element_type=jnp.float32)
    chosen = routes[:, :, None] == jnp.arange(expert_total, dtype=jnp.int32)[None, None, :]
    picked = jnp.sum(jnp.where(chosen, logits[:, None, :], 0.0), axis=2)
    sigmoids = jax.nn.sigmoid(picked)
    gate_values = sigmoids / jnp.sum(sigmoids, axis=1, keepdims=True)
    flag_table = chosen.reshape(length * top_count, expert_total).astype(jnp.int32)
    slot_index = jnp.sum(flag_table * (jnp.cumsum(flag_table, axis=0) - 1), axis=1)
    flat_routes = routes.reshape(-1)
    destination = (
        flat_routes % local_count * groups + flat_routes // local_count
    ) * capacity + slot_index
    copies = jnp.broadcast_to(features[:, None, :], (length, top_count, model_width)).reshape(
        -1, model_width
    )
    dispatch = (
        jnp.zeros((local_count * groups * capacity, model_width), jnp.bfloat16)
        .at[destination]
        .set(copies)
    )
    dispatch = dispatch.reshape(local_count, groups, capacity, model_width)
    arrived = lax.all_to_all(dispatch, "exp", split_axis=1, concat_axis=1, tiled=True)
    arrived = arrived.reshape(local_count, groups * capacity, model_width)
    gate_up = jnp.einsum(
        "erd,edf->erf",
        arrived,
        lax.all_gather(expert_gate_up, "ctx", axis=1, tiled=True),
        preferred_element_type=jnp.float32,
    )
    hidden = (jax.nn.silu(gate_up[..., :hidden_units]) * gate_up[..., hidden_units:]).astype(
        jnp.bfloat16
    )
    produced = jnp.einsum(
        "erf,efd->erd",
        hidden,
        lax.all_gather(expert_down, "ctx", axis=1, tiled=True),
        preferred_element_type=jnp.float32,
    )
    produced = produced.astype(jnp.bfloat16)
    returned = lax.all_to_all(
        produced.reshape(local_count, groups, capacity, model_width),
        "exp",
        split_axis=1,
        concat_axis=1,
        tiled=True,
    )
    results = returned.reshape(-1, model_width)[destination].reshape(length, top_count, model_width)
    routed_output = jnp.einsum("tk,tkd->td", gate_values, results.astype(jnp.float32))
    shared_units = shared_down.shape[0]
    shared_product = jnp.dot(features, shared_gate_up, preferred_element_type=jnp.float32)
    shared_hidden = (
        jax.nn.silu(shared_product[:, :shared_units]) * shared_product[:, shared_units:]
    ).astype(jnp.bfloat16)
    shared_expert_output = jnp.dot(shared_hidden, shared_down, preferred_element_type=jnp.float32)
    mixer_input_rows = (features.astype(jnp.float32) + shared_expert_output + routed_output).astype(
        jnp.bfloat16
    )
    head_count = decay_rate.shape[0]
    head_dim = model_width // head_count
    state_size = state_input_vectors.shape[2]
    block_rows = min(128, length)
    block_count = length // block_rows
    values = mixer_input_rows.astype(jnp.float32).reshape(length, head_count, head_dim)
    step_sizes = jax.nn.softplus(step_sizes_unsoftened[0])
    writes = state_input_vectors[0].astype(jnp.float32)
    read_vectors = state_output_vectors[0].astype(jnp.float32)
    upstream = cotangent[0].astype(jnp.float32).reshape(length, head_count, head_dim)
    lengths_row = document_length_table[0]
    starts = jnp.cumsum(lengths_row) - lengths_row
    offset = lax.axis_index("ctx") * length
    positions = offset + jnp.arange(length, dtype=jnp.int32)
    documents = document_index(starts, positions)
    before = document_index(starts, positions - 1)
    block_writes = state_input_vectors[0].reshape(block_count, block_rows, state_size)
    block_reads = state_output_vectors[0].reshape(block_count, block_rows, state_size)
    inputs = (
        values.reshape(block_count, block_rows, head_count, head_dim),
        step_sizes.reshape(block_count, block_rows, head_count),
        block_writes,
        block_reads,
        documents.reshape(block_count, block_rows),
        before.reshape(block_count, block_rows)[:, 0],
    )

    def advance(carry_state, block_inputs):
        return state_block(carry_state, block_inputs, decay_rate)

    initial = jnp.zeros((head_count, head_dim, state_size), jnp.float32)
    local_state, (outputs, weights, carried, closing, keep_factor) = lax.scan(
        advance, initial, inputs
    )

    def retreat(grad_state, block_inputs):
        weight_block, seed_block, carry_weight, close_weight, keep_block, write_half, read_half = (
            block_inputs
        )
        write_block = write_half.astype(jnp.float32)
        read_block = read_half.astype(jnp.float32)
        back_term = jnp.einsum("hts,thp->shp", weight_block, seed_block, precision=highest)
        back_term = back_term + close_weight[:, :, None] * jnp.einsum(
            "hpn,sn->shp", grad_state, write_block, precision=highest
        )
        grad_state = keep_block[:, None, None] * grad_state + jnp.einsum(
            "th,thp,tn->hpn", carry_weight, seed_block, read_block, precision=highest
        )
        return (grad_state, back_term)

    local_grad, back_terms = lax.scan(
        retreat,
        initial,
        (
            weights,
            upstream.reshape(block_count, block_rows, head_count, head_dim),
            carried,
            closing,
            keep_factor,
            block_writes,
            block_reads,
        ),
        reverse=True,
    )
    cumulative = jnp.cumsum(-step_sizes * decay_rate[None, :], axis=0)
    keep_all = jnp.exp(cumulative[-1]) * (documents[-1] == before[0]).astype(jnp.float32)
    identity = (jnp.ones_like(keep_all), jnp.zeros_like(local_state))
    entering = carried_in((keep_all, local_state), "ctx", combine_states, identity, False)[1]
    leaving = carried_in((keep_all, local_grad), "ctx", combine_states, identity, True)[1]
    entry_weight = jnp.exp(cumulative) * (documents == before[0]).astype(jnp.float32)[:, None]
    exit_weight = (
        jnp.exp(cumulative[-1][None, :] - cumulative)
        * (documents == documents[-1]).astype(jnp.float32)[:, None]
        * step_sizes
    )
    result = outputs.reshape(length, head_count, head_dim)
    result = result + entry_weight[:, :, None] * jnp.einsum(
        "hpn,tn->thp", entering, read_vectors, precision=highest
    )
    result = result + skip_gain[None, :, None] * values
    gradient = back_terms.reshape(length, head_count, head_dim)
    gradient = gradient + exit_weight[:, :, None] * jnp.einsum(
        "hpn,sn->shp", leaving, writes, precision=highest
    )
    gradient = gradient + skip_gain[None, :, None] * upstream
    return (
        result.reshape(1, length, model_width).astype(jnp.bfloat16),
        gradient.reshape(1, length, model_width).astype(jnp.bfloat16),
    )


def solution(mesh):
    return jax.shard_map(
        on_device,
        mesh=mesh,
        in_specs=(
            P("exp", "ctx", None),
            P(),
            P("exp", "ctx", None),
            P("exp", "ctx", None),
            P(),
            P(),
            P("exp", "ctx", None),
            P("exp", None),
            P("exp", "ctx", None),
            P("exp", "ctx", None),
            P("exp", "ctx", None),
            P(),
            P(),
            P("exp", "ctx", None),
        ),
        out_specs=(P("exp", "ctx", None), P("exp", "ctx", None)),
        check_vma=False,
    )
```

profile of v0, /device:TPU:27, one launch (start us, length us, event | category | flops | bytes accessed | tf_op | source)
XLA Modules:
  0.0 573.4 jit_solution(14089314108795506633)
XLA Ops:
  10.4 31.1 %reduce-window.9 = s32[64,8,128]{2,1,0:T(8,128)S(1)} reduce-window(s32[64,8,128]{2,1,0:T(8,128)} %fusion.47, s32[]{:T(128)} %constant.154.clone.1), window={size=1x1x128 pad=0_0x0_0x127_0}, to_apply=%region_2.3 | reduce-window | flops 8323072 | bytes 524292 | tf_op jit(solution)/shard_map/reduce-window
  45.9 11.6 %scatter_custom_fusion = bf16[1280,2560]{1,0:T(8,128)(2,1)} fusion(s32[1024]{0:T(1024)S(1)} %bitcast.181, bf16[]{:T(256)} %constant.153.clone.1, bf16[128,2560]{1,0:T(8,128)(2,1)S(1)} %bitcast.165), kind=kCustom, calls=%fused_computation.11 | custom fusion | bytes 7208962 | tf_op jit(solution)/shard_map/scatter | solution.py:106
  57.4 9.7 %reshape.413 = bf16[2,32,20,2560]{3,2,1,0:T(8,128)(2,1)} reshape(bf16[1280,2560]{1,0:T(8,128)(2,1)} %scatter_custom_fusion) | data formatting | bytes 13107200 | tf_op jit(solution)/shard_map/reshape | solution.py:108
  67.1 11.0 %copy.79 = bf16[2,32,20,2560]{3,0,2,1:T(2,128)(2,1)} copy(bf16[2,32,20,2560]{3,2,1,0:T(8,128)(2,1)} %reshape.413) | data formatting | bytes 13107200 | tf_op jit(solution)/shard_map/reshape | solution.py:108
  78.2 11.2 %all-to-all-start = ((bf16[2,32,20,2560]{3,0,2,1:T(2,128)(2,1)}), bf16[2,32,20,2560]{3,0,2,1:T(2,128)(2,1)}, u32[]{:S(2)}, u32[]{:S(2)}) async-start(bf16[2,32,20,2560]{3,0,2,1:T(2,128)(2,1)} %copy.79), calls=%async_computation | async-start | bytes 13107200 | tf_op jit(solution)/shard_map/all_to_all | solution.py:109
  95.3 2.2 copy.91
  97.5 3.0 convolution_add_fusion.1
  100.5 138.3 %all-to-all-done = bf16[2,32,20,2560]{3,0,2,1:T(2,128)(2,1)} async-done(((bf16[2,32,20,2560]{3,0,2,1:T(2,128)(2,1)}), bf16[2,32,20,2560]{3,0,2,1:T(2,128)(2,1)}, u32[]{:S(2)}, u32[]{:S(2)}) %all-to-all-start) | async-done | bytes 6553632 | tf_op jit(solution)/shard_map/all_to_all | solution.py:109
  238.8 9.4 %fusion = f32[2,640,512]{2,1,0:T(8,128)} fusion(bf16[2,2560,512]{2,1,0:T(8,128)(2,1)} %all-gather.8.cloned.1.call-done, bf16[2,640,2560]{2,0,1:T(2,128)(2,1)} %bitcast.12), kind=kOutput, calls=%fused_computation.6 | convolution fusion | flops 3355443200 | bytes 14417920 | tf_op jit(solution)/shard_map/erd,edf->erf/dot_general | solution.py:111
  248.2 4.4 convolution_convert_fusion
  252.7 29.4 %copy.81 = bf16[2,640,2560]{2,0,1:T(2,128)(2,1)} copy(bf16[2,640,2560]{2,1,0:T(8,128)(2,1)S(1)} %convolution_convert_fusion) | data formatting | bytes 13107200 | tf_op jit(solution)/shard_map/convert_element_type | solution.py:126
  282.1 8.9 %all-to-all-start.1 = ((bf16[2,32,20,2560]{3,0,2,1:T(2,128)(2,1)}), bf16[2,32,20,2560]{3,0,2,1:T(2,128)(2,1)}, u32[]{:S(2)}, u32[]{:S(2)}) async-start(bf16[2,32,20,2560]{3,0,2,1:T(2,128)(2,1)} %bitcast.164), calls=%async_computation.1 | async-start | bytes 13107200 | tf_op jit(solution)/shard_map/all_to_all | solution.py:127
  294.2 146.4 %all-to-all-done.1 = bf16[2,32,20,2560]{3,0,2,1:T(2,128)(2,1)} async-done(((bf16[2,32,20,2560]{3,0,2,1:T(2,128)(2,1)}), bf16[2,32,20,2560]{3,0,2,1:T(2,128)(2,1)}, u32[]{:S(2)}, u32[]{:S(2)}) %all-to-all-start.1) | async-done | bytes 6553632 | tf_op jit(solution)/shard_map/all_to_all | solution.py:127
  440.5 7.1 %copy.82 = bf16[2,32,20,2560]{3,2,1,0:T(8,128)(2,1)} copy(bf16[2,32,20,2560]{3,0,2,1:T(2,128)(2,1)} %all-to-all-done.1) | data formatting | bytes 13107200 | tf_op jit(solution)/shard_map/all_to_all | solution.py:127
  447.7 9.9 %reshape.416 = bf16[1280,2560]{1,0:T(8,128)(2,1)} reshape(bf16[2,32,20,2560]{3,2,1,0:T(8,128)(2,1)} %copy.82) | data formatting | bytes 13107200 | tf_op jit(solution)/shard_map/reshape | solution.py:134
  457.5 14.1 %gather_fusion = bf16[1024,2560]{1,0:T(8,128)(2,1)} fusion(bf16[1280,2560]{1,0:T(8,128)(2,1)} %reshape.416, s32[1024]{0:T(1024)S(1)} %broadcast_clamp_fusion), kind=kCustom, calls=%fused_computation | custom fusion | bytes 10489856 | tf_op jit(solution)/shard_map/gather | solution.py:134
  471.7 4.1 fusion.2
  479.1 7.6 %all-gather.2 = f32[8,1,40]{2,1,0:T(1,128)S(1)} all-gather(f32[1,1,40]{2,1,0:T(1,128)S(1)} %get-tuple-element.239), channel_id=1, replica_groups=mesh['ctx'=8,'exp'=32] {'ctx'}, dimensions={0}, use_global_device_ids=true | all-gather | bytes 1440 | tf_op jit(solution)/shard_map/all_gather | solution.py:13
  486.9 2.0 fusion.23
  491.5 2.3 fusion.24
  494.9 2.9 fusion.22
  499.6 39.1 %all-gather.12.cloned.1.call-done = f32[320,64,128]{2,1,0:T(8,128)} async-done(((f32[40,64,128]{2,1,0:T(8,128)}), f32[320,64,128]{2,1,0:T(8,128)}) %all-gather.12.cloned.1.call-update) | async-done | bytes 10485776 | tf_op jit(solution)/shard_map/all_gather | solution.py:13
  540.0 21.1 %while.16 = (s32[]{:T(128)}, f32[40,64,128]{2,1,0:T(8,128)}, s32[]{:T(128)}, f32[8,40]{1,0:T(8,128)S(1)}, f32[8,40,64,128]{3,2,1,0:T(8,128)}, /*index=5*/s32[]{:T(128)}, s32[]{:T(128)}, s32[]{:T(128)}) while((s32[]{:T(128)}, f32[40,64,128]{2,1,0:T(8,128)}, s32[]{:T(128)}, f32[8,40]{1,0:T(8,128)S(1)}, f32[8,40,64,128]{3,2,1,0:T(8,128)}, ...), condition=%wide.region_11.12_spmd, body=%wide.region_10.11_spmd.sunk | while | flops 655365 | bytes 3932767 | solution.py:22
  540.0 3.0 bitcast_add_fusion.4
  543.0 3.0 bitcast_add_fusion.4
  546.1 3.0 bitcast_add_fusion.4
  549.1 3.0 bitcast_add_fusion.4
  552.1 3.0 bitcast_add_fusion.4
  555.1 3.0 bitcast_add_fusion.4
  558.1 3.0 bitcast_add_fusion.4
  561.2 3.5 fusion.25
  564.7 2.2 copy.92
  (102 shorter events, 25.3 us)
Async XLA Ops:
  7.2 285.8 %copy-start = (bf16[2560,512]{1,0:T(8,128)(2,1)S(1)}, bf16[2560,512]{1,0:T(8,128)(2,1)}, u32[]{:S(2)}) copy-start(bf16[2560,512]{1,0:T(8,128)(2,1)} %param.22) | copy-start | bytes 7864324
  7.2 93.3 %all-gather.8.cloned.1.call-start = ((), (), s32[]{:S(2)}) async-start(), calls=%async_computation.2 | async-start | bytes 5898240 | tf_op jit(solution)/shard_map/all_gather | solution.py:114
  8.8 37.0 %copy-start.2 = (bf16[1,128,2560]{2,1,0:T(8,128)(2,1)S(1)}, bf16[1,128,2560]{2,1,0:T(8,128)(2,1)}, u32[]{:S(2)}) copy-start(bf16[1,128,2560]{2,1,0:T(8,128)(2,1)} %param.18) | copy-start | bytes 1966084
  78.2 12.2 %copy-start.16 = (s32[1,8]{1,0:T(1,128)S(1)}, s32[1,8]{1,0:T(1,128)}, u32[]{:S(2)}) copy-start(s32[1,8]{1,0:T(1,128)} %param.25) | copy-start | bytes 100
  78.2 13.8 %copy-start.10 = (f32[1,128,40]{1,2,0:T(8,128)S(1)}, f32[1,128,40]{1,2,0:T(8,128)}, u32[]{:S(2)}) copy-start(f32[1,128,40]{1,2,0:T(8,128)} %param.26) | copy-start | bytes 61444
  78.2 14.5 %copy-start.15 = (f32[40]{0:T(128)S(1)}, f32[40]{0:T(128)}, u32[]{:S(2)}) copy-start(f32[40]{0:T(128)} %param.29) | copy-start | bytes 484
  78.2 160.6 %all-to-all-start = ((bf16[2,32,20,2560]{3,0,2,1:T(2,128)(2,1)}), bf16[2,32,20,2560]{3,0,2,1:T(2,128)(2,1)}, u32[]{:S(2)}, u32[]{:S(2)}) async-start(bf16[2,32,20,2560]{3,0,2,1:T(2,128)(2,1)} %copy.79), calls=%async_computation | async-start | bytes 13107200 | tf_op jit(solution)/shard_map/all_to_all | solution.py:109
  89.4 8.1 %copy-start.7 = (bf16[1,128,128]{2,1,0:T(8,128)(2,1)S(1)}, bf16[1,128,128]{2,1,0:T(8,128)(2,1)}, u32[]{:S(2)}) copy-start(bf16[1,128,128]{2,1,0:T(8,128)(2,1)} %param.28) | copy-start | bytes 98308
  89.4 158.8 %all-gather.10.cloned.1.call-start = ((), (), s32[]{:S(2)}) async-start(), calls=%async_computation.3 | async-start | bytes 2949120 | tf_op jit(solution)/shard_map/all_gather | solution.py:123
  90.2 400.5 %all-gather.14.cloned.1.call-start = ((), (), s32[]{:S(2)}) async-start(), calls=%async_computation.5 | async-start | bytes 11796480 | tf_op jit(solution)/shard_map/all_gather | solution.py:13
  282.1 10.6 %copy-start.13 = (s32[1,128,8]{1,2,0:T(8,128)S(1)}, s32[1,128,8]{1,2,0:T(8,128)}, u32[]{:S(2)}) copy-start(s32[1,128,8]{1,2,0:T(8,128)} %param.24) | copy-start | bytes 12292
  282.1 158.4 %all-to-all-start.1 = ((bf16[2,32,20,2560]{3,0,2,1:T(2,128)(2,1)}), bf16[2,32,20,2560]{3,0,2,1:T(2,128)(2,1)}, u32[]{:S(2)}, u32[]{:S(2)}) async-start(bf16[2,32,20,2560]{3,0,2,1:T(2,128)(2,1)} %bitcast.164), calls=%async_computation.1 | async-start | bytes 13107200 | tf_op jit(solution)/shard_map/all_to_all | solution.py:127
  291.0 247.7 %all-gather.12.cloned.1.call-start = ((), (), s32[]{:S(2)}) async-start(), calls=%async_computation.4 | async-start | bytes 11796480 | tf_op jit(solution)/shard_map/all_gather | solution.py:13
  471.7 4.1 copy-start.4
  471.7 4.1 copy-start.5
  476.2 0.8 copy-start.6
  476.9 1.9 copy-start.9
  476.9 2.1 copy-start.8
  478.8 8.1 %copy-start.3 = (bf16[1,128,2560]{1,2,0:T(8,128)(2,1)S(1)}, bf16[1,128,2560]{1,2,0:T(8,128)(2,1)}, u32[]{:S(2)}) copy-start(bf16[1,128,2560]{1,2,0:T(8,128)(2,1)} %copy.91) | copy-start | bytes 1966084
  479.0 9.9 %copy-start.11 = (f32[40,128]{1,0:T(8,128)}, f32[40,128]{1,0:T(8,128)S(1)}, u32[]{:S(2)}) copy-start(f32[40,128]{1,0:T(8,128)S(1)} %copy.85) | copy-start | bytes 61444
  490.8 0.7 copy-start.14
  493.8 1.1 copy-start.12
  561.2 5.7 copy-start.1
Sparse Core Ops, SparseCore 0:
  9.9 40.2 all-gather.7
  92.1 29.4 all-gather.9
  123.4 60.9 all-gather.13
  478.9 59.7 all-gather.11
where the time goes:
time: 576 us; the launch traced here: 573 us
  waiting for transfers between devices  325 us (56%)
  local copies, waits for them, and re-layouts  107 us (19%)
  other arithmetic  56.8 us (10%)
  matrix products  40.1 us (7%)
  starting transfers between devices  20.7 us (4%)
  between operations  15.4 us (3%)
  blocking collectives  7.6 us (1%)
    all_to_all x1, waiting for transfers between devices, on_device(): lax.all_to_all(produced.reshape(local_count, groups, capacity, model_widt...  146 us
    all_to_all x1, waiting for transfers between devices, on_device(): lax.all_to_all(dispatch, 'exp', split_axis=1, concat_axis=1, tiled=True)  138 us
    all_gather x2, waiting for transfers between devices, carried_in(): gathered = jax.tree.map(lambda a: lax.all_gather(a, axis), part)  39.1 us
    another operation x3, other arithmetic  31.4 us
    convert_element_type x1, local copies, waits for them, and re-layouts, on_device(): produced = produced.astype(jnp.bfloat16)  29.4 us
    add x7, other arithmetic, combine_states(): later[0][:, None, None] * earlier[1] + later[1]  21.1 us
    reshape x2, local copies, waits for them, and re-layouts, on_device(): dispatch = dispatch.reshape(local_count, groups, capacity, model_width)  20.7 us
    gather x1, local copies, waits for them, and re-layouts, on_device(): returned.reshape(-1, model_width)[destination]  14.1 us
  transfers between devices with their start and end apart: 6, of which 3 were waited for; matrix products, arithmetic and copies ran while one was open for 31% of the time, Pallas kernels for 0%

commit v1 on v0

--- a/solution.py
+++ b/solution.py
@@ -1,9 +1,346 @@
+import functools
+
 import jax
 import jax.numpy as jnp
 from jax import lax
+from jax.experimental import pallas as pl
+from jax.experimental.pallas import tpu as pltpu
 from jax.sharding import PartitionSpec as P
 
 highest = lax.Precision.HIGHEST
+MESH = pl.DeviceIdType.MESH
+F32 = jnp.float32
+BF16 = jnp.bfloat16
+
+T = 128
+D = 2560
+E = 64
+K = 8
+FH = 256
+NZ, NX, NY = 8, 4, 4
+GR = D // 8
+DR = FH // 8
+H = D // 2
+SLOT = {4: 0, 3: 1, -3: 2, 2: 3, -2: 4, 1: 5, -1: 6, 0: 7}
+
+
+def expert_kernel(
+    x_hbm, router_ref, gu_hbm, dn_hbm, sgu_ref, sdn_ref, idx_ref, out_ref,
+    xall, gall, wg, wd, hid, part, shared, rr, rl, sr, sl_, loc, ss, rs,
+):
+    ctx = lax.axis_index("ctx")
+    exp = lax.axis_index("exp")
+    z, x = exp // NX, exp % NX
+    y, core = ctx // 2, ctx % 2
+    zp = {"exp": (exp + NX) % (NX * NZ)}
+    zm = {"exp": (exp + NX * (NZ - 1)) % (NX * NZ)}
+    xp = {"exp": z * NX + (x + 1) % NX}
+    xm = {"exp": z * NX + (x + NX - 1) % NX}
+    yp = {"ctx": (ctx + 2) % 8}
+    ym = {"ctx": (ctx + 6) % 8}
+    sib = {"ctx": ctx + 1 - 2 * core}
+    y1, y2, y3 = (y + 1) % NY, (y + 2) % NY, (y + 3) % NY
+    other = 1 - core
+
+    counter = [0]
+
+    def rcopy(src, dst, dev, k):
+        return pltpu.make_async_remote_copy(
+            src_ref=src, dst_ref=dst, send_sem=ss.at[k], recv_sem=rs.at[k],
+            device_id=dev, device_id_type=MESH,
+        )
+
+    sent = []
+
+    def send(src, dst, dev):
+        k = counter[0]
+        counter[0] += 1
+        c = rcopy(src, dst, dev, k)
+        c.start()
+        sent.append(c)
+        return k
+
+    def arrived(k, region):
+        rcopy(region, region, sib, k).wait_recv()
+
+    barrier = pltpu.get_barrier_semaphore()
+    for dev in (zp, zm, xp, xm, yp, ym, sib):
+        pl.semaphore_signal(barrier, inc=1, device_id=dev, device_id_type=MESH)
+    pl.semaphore_wait(barrier, 7)
+
+    x_own = xall.at[SLOT[0]]
+    lx = pltpu.make_async_copy(x_hbm.at[0], x_own, loc.at[0])
+    lx.start()
+    kx = {}
+    kx[-1] = send(x_hbm.at[0], xall.at[SLOT[-1]], zp)
+    kx[1] = send(x_hbm.at[0], xall.at[SLOT[1]], zm)
+    own = {}
+    for name, hbm, w in (("g", gu_hbm, wg), ("d", dn_hbm, wd)):
+        own[name, "A", 2] = send(hbm.at[0], w.at[2, 0, y, core], xp)
+        own[name, "A", 1] = send(hbm.at[0], w.at[1, 0, y, core], xm)
+        own[name, "B", 3] = send(hbm.at[1], w.at[0, 1, y, core], yp)
+        own[name, "B", 1] = send(hbm.at[1], w.at[0, 1, y, core], ym)
+        own[name, "S"] = send(hbm, w.at[0, :, y, core], sib)
+    lg = pltpu.make_async_copy(gu_hbm, wg.at[0, :, y, core], loc.at[1])
+    ld = pltpu.make_async_copy(dn_hbm, wd.at[0, :, y, core], loc.at[2])
+    lg.start()
+    ld.start()
+
+    lx.wait()
+    xo = x_own[...]
+    logits = jnp.dot(xo, router_ref[...], preferred_element_type=F32)
+    lane = lax.broadcasted_iota(jnp.int32, (T, E), 1)
+    chosen = jnp.zeros((T, E), F32)
+    idx = idx_ref[0]
+    for j in range(K):
+        chosen = chosen + jnp.where(idx[:, j : j + 1] == lane, 1.0, 0.0)
+    sig = chosen * jax.nn.sigmoid(logits)
+    gate = sig / jnp.sum(sig, axis=1, keepdims=True)
+    hi = gate.astype(BF16)
+    lo = (gate - hi.astype(F32)).astype(BF16)
+    gall[SLOT[0], :, 0:E] = hi
+    gall[SLOT[0], :, E : 2 * E] = lo
+    kg = {}
+    kg[-1] = send(gall.at[SLOT[0]], gall.at[SLOT[-1]], zp)
+    kg[1] = send(gall.at[SLOT[0]], gall.at[SLOT[1]], zm)
+
+    sp = jnp.dot(xo, sgu_ref[...], preferred_element_type=F32)
+    sh = (jax.nn.silu(sp[:, :FH]) * sp[:, FH:]).astype(BF16)
+    shared[...] = xo.astype(F32) + jnp.dot(sh, sdn_ref[...], preferred_element_type=F32)
+
+    half = {}
+    row = {"g": (wg, GR), "d": (wd, DR)}
+
+    def first_ring(name):
+        w, n = row[name]
+        h = n // 2
+        lo_, hi_ = pl.ds(0, h), pl.ds(h, h)
+        arrived(own[name, "A", 2], w.at[2, 0, y, core])
+        half[name, "A", 2] = send(w.at[2, 0, y, core, lo_], w.at[3, 0, y, core, lo_], xp)
+        arrived(own[name, "A", 1], w.at[1, 0, y, core])
+        half[name, "A", 1] = send(w.at[1, 0, y, core, hi_], w.at[3, 0, y, core, hi_], xm)
+        arrived(own[name, "B", 3], w.at[0, 1, y3, core])
+        half[name, "B", 3] = send(w.at[0, 1, y3, core, lo_], w.at[0, 1, y3, core, lo_], yp)
+        arrived(own[name, "B", 1], w.at[0, 1, y1, core])
+        half[name, "B", 1] = send(w.at[0, 1, y1, core, hi_], w.at[0, 1, y1, core, hi_], ym)
+        own[name, "B", 3, "S"] = send(w.at[0, 1, y3, core], w.at[0, 1, y3, core], sib)
+        own[name, "B", 1, "S"] = send(w.at[0, 1, y1, core], w.at[0, 1, y1, core], sib)
+
+    slab = {}
+
+    def second_ring(name):
+        w, n = row[name]
+        h = n // 2
+        lo_, hi_ = pl.ds(0, h), pl.ds(h, h)
+        arrived(half[name, "A", 2], w.at[3, 0, y, core, lo_])
+        arrived(half[name, "A", 1], w.at[3, 0, y, core, hi_])
+        a = w.at[:, 0, y, core]
+        slab[name, "A", 3] = send(a, a, yp)
+        slab[name, "A", 1] = send(a, a, ym)
+        arrived(half[name, "B", 3], w.at[0, 1, y2, core, lo_])
+        arrived(half[name, "B", 1], w.at[0, 1, y2, core, hi_])
+        b = w.at[0, 1, :, core]
+        slab[name, "B", 2] = send(b, w.at[2, 1, :, core], xp)
+        slab[name, "B", 1] = send(b, w.at[1, 1, :, core], xm)
+        s = w.at[pl.ds(1, 3), 0, y, core]
+        slab[name, "A", 0, "S"] = send(s, s, sib)
+        s = w.at[0, 1, y2, core]
+        slab[name, "B", 0, "S"] = send(s, s, sib)
+
+    last = {}
+
+    def third(name):
+        w, n = row[name]
+        a3, a1 = w.at[:, 0, y3, core], w.at[:, 0, y1, core]
+        arrived(slab[name, "A", 3], a3)
+        s = w.at[pl.ds(0, 2), 0, y3, core]
+        last[name, "A", 3] = send(s, s, yp)
+        arrived(slab[name, "A", 1], a1)
+        s = w.at[pl.ds(2, 2), 0, y1, core]
+        last[name, "A", 1] = send(s, s, ym)
+        b2, b1 = w.at[2, 1, :, core], w.at[1, 1, :, core]
+        arrived(slab[name, "B", 2], b2)
+        last[name, "B", 2] = send(w.at[2, 1, pl.ds(0, 2), core], w.at[3, 1, pl.ds(0, 2), core], xp)
+        arrived(slab[name, "B", 1], b1)
+        last[name, "B", 1] = send(w.at[1, 1, pl.ds(2, 2), core], w.at[3, 1, pl.ds(2, 2), core], xm)
+        for key, s in (("A3", a3), ("A1", a1), ("B2", b2), ("B1", b1)):
+            last[name, key, "S"] = send(s, s, sib)
+
+    fin = {}
+
+    def fourth(name):
+        w, n = row[name]
+        arrived(last[name, "A", 3], w.at[pl.ds(0, 2), 0, y2, core])
+        arrived(last[name, "A", 1], w.at[pl.ds(2, 2), 0, y2, core])
+        s = w.at[:, 0, y2, core]
+        fin[name, "A", "S"] = send(s, s, sib)
+        arrived(last[name, "B", 2], w.at[3, 1, pl.ds(0, 2), core])
+        arrived(last[name, "B", 1], w.at[3, 1, pl.ds(2, 2), core])
+        s = w.at[3, 1, :, core]
+        fin[name, "B", "S"] = send(s, s, sib)
+
+    def from_sibling(name):
+        w, n = row[name]
+        arrived(own[name, "S"], w.at[0, :, y, other])
+        arrived(own[name, "B", 3, "S"], w.at[0, 1, y3, other])
+        arrived(own[name, "B", 1, "S"], w.at[0, 1, y1, other])
+        arrived(slab[name, "A", 0, "S"], w.at[pl.ds(1, 3), 0, y, other])
+        arrived(slab[name, "B", 0, "S"], w.at[0, 1, y2, other])
+        arrived(last[name, "A3", "S"], w.at[:, 0, y3, other])
+        arrived(last[name, "A1", "S"], w.at[:, 0, y1, other])
+        arrived(last[name, "B2", "S"], w.at[2, 1, :, other])
+        arrived(last[name, "B1", "S"], w.at[1, 1, :, other])
+        arrived(fin[name, "A", "S"], w.at[:, 0, y2, other])
+        arrived(fin[name, "B", "S"], w.at[3, 1, :, other])
+
+    def token_step(d):
+        for buf, keys in ((xall, kx), (gall, kg)):
+            arrived(keys[-d], buf.at[SLOT[-d]])
+            arrived(keys[d], buf.at[SLOT[d]])
+            if d < 3:
+                keys[-d - 1] = send(buf.at[SLOT[-d]], buf.at[SLOT[-d - 1]], zp)
+                keys[d + 1] = send(buf.at[SLOT[d]], buf.at[SLOT[d + 1]], zm)
+            else:
+                lo_, hi_ = pl.ds(0, T // 2), pl.ds(T // 2, T // 2)
+                keys["lo"] = send(buf.at[SLOT[-3], lo_], buf.at[SLOT[4], lo_], zp)
+                keys["hi"] = send(buf.at[SLOT[3], hi_], buf.at[SLOT[4], hi_], zm)
+
+    lg.wait()
+    ld.wait()
+    first_ring("g")
+    second_ring("g")
+    token_step(1)
+    first_ring("d")
+    second_ring("d")
+    token_step(2)
+    third("g")
+    token_step(3)
+    for buf, keys in ((xall, kx), (gall, kg)):
+        arrived(keys["lo"], buf.at[SLOT[4], pl.ds(0, T // 2)])
+        arrived(keys["hi"], buf.at[SLOT[4], pl.ds(T // 2, T // 2)])
+    fourth("g")
+    from_sibling("g")
+
+    MT = 256
+
+    def hidden(n, _):
+        slot, e = n // 2, n % 2
+        expert = 2 * (z * NX + (x + jnp.where(slot == 2, 3, jnp.where(slot == 3, 2, slot))) % NX) + e
+        r = lax.broadcasted_iota(jnp.int32, (2 * E, FH), 0)
+        sel = jnp.where((r == expert) | (r == expert + E), 1.0, 0.0).astype(BF16)
+
+        def tile(m, _):
+            xs = xall[pl.ds(m * (MT // T), MT // T)].reshape(MT, D)
+            gs = gall[pl.ds(m * (MT // T), MT // T)].reshape(MT, 2 * E)
+            w = wg[slot, e].reshape(D, 2 * FH)
+            p = jnp.dot(xs, w, preferred_element_type=F32)
+            g = jnp.dot(gs, sel, preferred_element_type=F32)
+            h = (jax.nn.silu(p[:, :FH]) * p[:, FH:] * g).astype(BF16)
+            hid[slot, e, pl.ds(pl.multiple_of(m * MT, MT), MT), :] = h
+            return 0
+
+        lax.fori_loop(0, NZ * T // MT, tile, 0)
+        return 0
+
+    lax.fori_loop(0, 4, hidden, 0)
+    third("d")
+    lax.fori_loop(4, 8, hidden, 0)
+    fourth("d")
+    from_sibling("d")
+
+    NC = 256
+
+    def partial(first, rows):
+        def tile(c, _):
+            cols = pl.ds(pl.multiple_of(c * NC, NC), NC)
+            acc = jnp.zeros((rows, NC), F32)
+            for slot in range(4):
+                for e in range(2):
+                    acc = acc + jnp.dot(
+                        hid[slot, e, pl.ds(first * T, rows), :],
+                        wd[slot, e, :, :, :, cols].reshape(FH, NC),
+                        preferred_element_type=F32,
+                    )
+            part[pl.ds(0, rows), cols] = acc
+            return 0
+
+        lax.fori_loop(0, D // NC, tile, 0)
+
+    c0, c1 = pl.ds(0, H), pl.ds(H, H)
+    kr, kl = {}, {}
+    partial(SLOT[4], T)
+    sr[0] = part[0:T, c0].astype(BF16)
+    kr[0] = send(sr.at[0], rr.at[0], zp)
+    sl_[0] = part[0:T, c1].astype(BF16)
+    kl[0] = send(sl_.at[0], rl.at[0], zm)
+    partial(SLOT[3], 2 * T)
+    sr[1] = part[0:T, c1].astype(BF16)
+    kr[1] = send(sr.at[1], rr.at[1], zp)
+    sl_[1] = part[T : 2 * T, c0].astype(BF16)
+    kl[1] = send(sl_.at[1], rl.at[1], zm)
+
+    def relay(k, cr, cl):
+        arrived(kr[k], rr.at[k])
+        rr[k] = (rr[k].astype(F32) + part[0:T, cr]).astype(BF16)
+        kr[k + 2] = send(rr.at[k], rr.at[k + 2], zp)
+        arrived(kl[k], rl.at[k])
+        rl[k] = (rl[k].astype(F32) + part[T : 2 * T, cl]).astype(BF16)
+        kl[k + 2] = send(rl.at[k], rl.at[k + 2], zm)
+
+    relay(0, c0, c1)
+    partial(SLOT[2], 2 * T)
+    relay(1, c1, c0)
+    relay(2, c0, c1)
+    partial(SLOT[1], 2 * T)
+    relay(3, c1, c0)
+    relay(4, c0, c1)
+    partial(SLOT[0], T)
+    for k, cr, cl in ((5, c1, c0), (6, c0, c1)):
+        arrived(kr[k], rr.at[k])
+        arrived(kl[k], rl.at[k])
+        part[0:T, cr] += rr[k].astype(F32)
+        part[0:T, cl] += rl[k].astype(F32)
+    out_ref[...] = (part[0:T, :] + shared[...]).astype(BF16)
+    for c in sent:
+        c.wait_send()
+
+
+COPIES = 2 + 10 + 2 + 2 * (6 + 6 + 8 + 2) + 12 + 14
+
+
+def routed_and_shared(tokens, router, gate_up, down, shared_gate_up, shared_down, routes):
+    vmem = pl.BlockSpec(memory_space=pltpu.VMEM)
+    hbm = pl.BlockSpec(memory_space=pl.ANY)
+    return pl.pallas_call(
+        expert_kernel,
+        out_shape=jax.ShapeDtypeStruct((T, D), BF16),
+        in_specs=[hbm, vmem, hbm, hbm, vmem, vmem, vmem],
+        out_specs=vmem,
+        scratch_shapes=[
+            pltpu.VMEM((NZ, T, D), BF16),
+            pltpu.VMEM((NZ, T, 2 * E), BF16),
+            pltpu.VMEM((NX, 2, NY, 2, GR, 2 * FH), BF16),
+            pltpu.VMEM((NX, 2, NY, 2, DR, D), BF16),
+            pltpu.VMEM((NX, 2, NZ * T, FH), BF16),
+            pltpu.VMEM((2 * T, D), F32),
+            pltpu.VMEM((T, D), F32),
+            pltpu.VMEM((7, T, H), BF16),
+            pltpu.VMEM((7, T, H), BF16),
+            pltpu.VMEM((2, T, H), BF16),
+            pltpu.VMEM((2, T, H), BF16),
+            pltpu.SemaphoreType.DMA((3,)),
+            pltpu.SemaphoreType.DMA((COPIES,)),
+            pltpu.SemaphoreType.DMA((COPIES,)),
+        ],
+        compiler_params=pltpu.CompilerParams(
+            collective_id=0, has_side_effects=True, vmem_limit_bytes=62 * 2**20
+        ),
+    )(tokens, router, gate_up, down, shared_gate_up, shared_down, routes)
+
+
+def running_sum(a):
+    lower = jnp.tril(jnp.ones((a.shape[0], a.shape[0]), F32))
+    return jnp.dot(lower, a, precision=highest)
 
 
 def carried_in(part, axis, combine, identity, reverse):
@@ -30,7 +367,7 @@
     values, step_sizes, write_half, read_half, documents, before = block_inputs
     writes = write_half.astype(jnp.float32)
     read_vectors = read_half.astype(jnp.float32)
-    cumulative = jnp.cumsum(-step_sizes * decay_rate[None, :], axis=0)
+    cumulative = running_sum(-step_sizes * decay_rate[None, :])
     token_order = jnp.arange(documents.shape[0], dtype=jnp.int32)
     causal = (documents[:, None] == documents[None, :]) & (
         token_order[:, None] >= token_order[None, :]
@@ -79,68 +416,8 @@
     features = tokens[0]
     length = features.shape[0]
     model_width = features.shape[1]
-    groups = lax.axis_size("exp")
-    local_count = expert_gate_up.shape[0]
-    expert_total = router.shape[1]
-    top_count = expert_index_table.shape[2]
-    capacity = 5 * length * top_count // (4 * expert_total)
-    hidden_units = expert_gate_up.shape[2] // 2
-    routes = expert_index_table[0]
-    logits = jnp.dot(features, router, preferred_element_type=jnp.float32)
-    chosen = routes[:, :, None] == jnp.arange(expert_total, dtype=jnp.int32)[None, None, :]
-    picked = jnp.sum(jnp.where(chosen, logits[:, None, :], 0.0), axis=2)
-    sigmoids = jax.nn.sigmoid(picked)
-    gate_values = sigmoids / jnp.sum(sigmoids, axis=1, keepdims=True)
-    flag_table = chosen.reshape(length * top_count, expert_total).astype(jnp.int32)
-    slot_index = jnp.sum(flag_table * (jnp.cumsum(flag_table, axis=0) - 1), axis=1)
-    flat_routes = routes.reshape(-1)
-    destination = (
-        flat_routes % local_count * groups + flat_routes // local_count
-    ) * capacity + slot_index
-    copies = jnp.broadcast_to(features[:, None, :], (length, top_count, model_width)).reshape(
-        -1, model_width
-    )
-    dispatch = (
-        jnp.zeros((local_count * groups * capacity, model_width), jnp.bfloat16)
-        .at[destination]
-        .set(copies)
-    )
-    dispatch = dispatch.reshape(local_count, groups, capacity, model_width)
-    arrived = lax.all_to_all(dispatch, "exp", split_axis=1, concat_axis=1, tiled=True)
-    arrived = arrived.reshape(local_count, groups * capacity, model_width)
-    gate_up = jnp.einsum(
-        "erd,edf->erf",
-        arrived,
-        lax.all_gather(expert_gate_up, "ctx", axis=1, tiled=True),
-        preferred_element_type=jnp.float32,
-    )
-    hidden = (jax.nn.silu(gate_up[..., :hidden_units]) * gate_up[..., hidden_units:]).astype(
-        jnp.bfloat16
-    )
-    produced = jnp.einsum(
-        "erf,efd->erd",
-        hidden,
-        lax.all_gather(expert_down, "ctx", axis=1, tiled=True),
-        preferred_element_type=jnp.float32,
-    )
-    produced = produced.astype(jnp.bfloat16)
-    returned = lax.all_to_all(
-        produced.reshape(local_count, groups, capacity, model_width),
-        "exp",
-        split_axis=1,
-        concat_axis=1,
-        tiled=True,
-    )
-    results = returned.reshape(-1, model_width)[destination].reshape(length, top_count, model_width)
-    routed_output = jnp.einsum("tk,tkd->td", gate_values, results.astype(jnp.float32))
-    shared_units = shared_down.shape[0]
-    shared_product = jnp.dot(features, shared_gate_up, preferred_element_type=jnp.float32)
-    shared_hidden = (
-        jax.nn.silu(shared_product[:, :shared_units]) * shared_product[:, shared_units:]
-    ).astype(jnp.bfloat16)
-    shared_expert_output = jnp.dot(shared_hidden, shared_down, preferred_element_type=jnp.float32)
-    mixer_input_rows = (features.astype(jnp.float32) + shared_expert_output + routed_output).astype(
-        jnp.bfloat16
+    mixer_input_rows = routed_and_shared(
+        tokens, router, expert_gate_up, expert_down, shared_gate_up, shared_down, expert_index_table
     )
     head_count = decay_rate.shape[0]
     head_dim = model_width // head_count
@@ -206,7 +483,7 @@
         ),
         reverse=True,
     )
-    cumulative = jnp.cumsum(-step_sizes * decay_rate[None, :], axis=0)
+    cumulative = running_sum(-step_sizes * decay_rate[None, :])
     keep_all = jnp.exp(cumulative[-1]) * (documents[-1] == before[0]).astype(jnp.float32)
     identity = (jnp.ones_like(keep_all), jnp.zeros_like(local_state))
     entering = carried_in((keep_all, local_state), "ctx", combine_states, identity, False)[1]

time: 576 us -> 324 us (0.56)
  waiting for transfers between devices: 325 us -> 36.4 us
  Pallas kernels: 0 us -> 216 us
  local copies, waits for them, and re-layouts: 107 us -> 14.4 us
  other arithmetic: 56.8 us -> 14.2 us
  matrix products: 40.1 us -> 16.6 us
  starting transfers between devices: 20.7 us -> 0.08 us
    all_to_all x2 -> x0, waiting for transfers between devices: 285 us -> none  [the longest x1 146 us: on_device(): lax.all_to_all(produced.reshape(local_count, groups, capacity, model_widt...]
    pallas_call x0 -> x1, Pallas kernels: none -> 216 us  [routed_and_shared(): pl.pallas_call(expert_kernel, out_shape=jax.ShapeDtypeStruct((T, D), BF16...]
    another operation x4 -> x1, other arithmetic: 31.5 us -> 0.83 us
    reshape x3 -> x0, local copies, waits for them, and re-layouts: 30.6 us -> none  [the longest x2 20.7 us: on_device(): dispatch = dispatch.reshape(local_count, groups, capacity, model_width)]
    convert_element_type x2 -> x0, local copies, waits for them, and re-layouts: 29.7 us -> none  [the longest x1 29.4 us: on_device(): produced = produced.astype(jnp.bfloat16)]
    dot_general x6 -> x1, matrix products: 20.9 us -> 0.27 us  [running_sum(): return jnp.dot(lower, a, precision=highest)]
    all_to_all x2 -> x0, starting transfers between devices: 20.1 us -> none  [the longest x1 11.2 us: on_device(): lax.all_to_all(dispatch, 'exp', split_axis=1, concat_axis=1, tiled=True)]
    gather x1 -> x0, local copies, waits for them, and re-layouts: 14.1 us -> none  [on_device(): returned.reshape(-1, model_width)[destination]]
  transfers between devices with their start and end apart: 6 -> 2, of which waited for: 3 -> 1; matrix products, arithmetic and copies ran while one was open for 31% -> 5% of each run, Pallas kernels for 0% -> 67%
where the time goes in v1:
time: 324 us; the launch traced here: 323 us
  Pallas kernels  216 us (67%)
  waiting for transfers between devices  36.4 us (11%)
  matrix products  16.6 us (5%)
  between operations  15.6 us (5%)
  local copies, waits for them, and re-layouts  14.4 us (4%)
  other arithmetic  14.2 us (4%)
  blocking collectives  10.2 us (3%)
    pallas_call x1, Pallas kernels, routed_and_shared(): pl.pallas_call(expert_kernel, out_shape=jax.ShapeDtypeStruct((T, D), BF16...  216 us
    all_gather x2, waiting for transfers between devices, carried_in(): gathered = jax.tree.map(lambda a: lax.all_gather(a, axis), part)  36.4 us
    add x7, other arithmetic, combine_states(): later[0][:, None, None] * earlier[1] + later[1]  11 us
    all_gather x1, blocking collectives, carried_in(): gathered = jax.tree.map(lambda a: lax.all_gather(a, axis), part)  10.2 us
    unnamed x31, local copies, waits for them, and re-layouts  7.21 us
  transfers between devices with their start and end apart: 2, of which 1 were waited for; matrix products, arithmetic and copies ran while one was open for 5% of the time, Pallas kernels for 67%

profile of v1, /device:TPU:27, one launch (start us, length us, event | category | flops | bytes accessed | tf_op | source)
XLA Modules:
  0.0 323.5 jit_solution(14794912290510166478)
XLA Ops:
  7.3 0.8 reduce-window_clone.1
  11.4 1.4 copy.38
  14.0 1.9 convolution_add_fusion
  15.9 1.1 copy.35.router_ref
  17.0 0.7 copy.36.idx_ref
  17.8 215.7 %shard_map.149 = bf16[128,2560]{1,0:T(8,128)(2,1)} custom-call(bf16[1,128,2560]{2,1,0:T(8,128)(2,1)} %x_hbm.1, bf16[2560,64]{1,0:T(8,128)(2,1)} %copy.35.router_ref, bf16[2,320,512]{2,1,0:T(8,128)(2,1)} %gu_hbm.1, bf16[2,32,2560]{2,1,0:T(8,128)(2,1)} %dn_hbm.1, bf16[2560,512]{1,0:T(8,128)(2,1)} %sgu_ref.1, bf16[256,2560]{1,0:T(8,128)(2,1)} %sdn_ref.1, ...), custom_call_target="tpu_custom_call" | custom-call | tf_op jit(solution)/shard_map/pallas_call | solution.py:314
  233.5 1.4 copy.37
  234.9 1.9 convolution_add_fusion.1
  236.8 10.2 %all-gather.2 = f32[8,1,40]{2,1,0:T(1,128)S(1)} all-gather(f32[1,1,40]{2,1,0:T(1,128)S(1)} %bitcast.132), channel_id=1, replica_groups=mesh['ctx'=8,'exp'=32] {'ctx'}, dimensions={0}, use_global_device_ids=true | all-gather | bytes 1440 | tf_op jit(solution)/shard_map/all_gather | solution.py:350
  247.2 3.0 fusion.12
  250.2 2.0 fusion.13
  252.2 1.8 fusion.5
  254.1 1.8 fusion.9
  256.8 2.2 fusion.14
  258.9 1.1 copy.40
  260.0 36.4 %all-gather.6.cloned.1.call-done = f32[320,64,128]{2,1,0:T(8,128)} async-done(((f32[40,64,128]{2,1,0:T(8,128)}), f32[320,64,128]{2,1,0:T(8,128)}) %all-gather.6.cloned.1.call-update) | async-done | bytes 10485776 | tf_op jit(solution)/shard_map/all_gather | solution.py:350
  296.6 16.2 %while.16 = (s32[]{:T(128)}, f32[40,64,128]{2,1,0:T(8,128)S(1)}, s32[]{:T(128)}, f32[8,40]{1,0:T(8,128)}, f32[8,40,64,128]{3,2,1,0:T(8,128)}, /*index=5*/s32[]{:T(128)}, s32[]{:T(128)}, s32[]{:T(128)}) while((s32[]{:T(128)}, f32[40,64,128]{2,1,0:T(8,128)S(1)}, s32[]{:T(128)}, f32[8,40]{1,0:T(8,128)}, f32[8,40,64,128]{3,2,1,0:T(8,128)}, ...), condition=%wide.region_4.5_spmd, body=%wide.region_3.4_spmd.sunk | while | flops 655365 | bytes 3932767 | solution.py:359
  296.6 0.8 dynamic-slice_bitcast_fusion.4
  297.4 1.6 bitcast_add_fusion.4
  299.0 0.7 dynamic-slice_bitcast_fusion.4
  299.7 1.6 bitcast_add_fusion.4
  301.3 0.7 dynamic-slice_bitcast_fusion.4
  302.0 1.6 bitcast_add_fusion.4
  303.6 0.7 dynamic-slice_bitcast_fusion.4
  304.3 1.6 bitcast_add_fusion.4
  305.9 0.7 dynamic-slice_bitcast_fusion.4
  306.6 1.6 bitcast_add_fusion.4
  308.9 1.6 bitcast_add_fusion.4
  310.5 0.7 dynamic-slice_bitcast_fusion.4
  311.2 1.6 bitcast_add_fusion.4
  312.8 1.7 fusion.15
  314.5 2.2 copy.39
  (48 shorter events, 5.2 us)
Async XLA Ops:
  7.2 227.8 %copy-start = (bf16[1,128,128]{2,1,0:T(8,128)(2,1)S(1)}, bf16[1,128,128]{2,1,0:T(8,128)(2,1)}, u32[]{:S(2)}) copy-start(bf16[1,128,128]{2,1,0:T(8,128)(2,1)} %param.27) | copy-start | bytes 98308
  7.2 5.7 %copy-start.7 = (f32[1,128,40]{1,2,0:T(8,128)S(1)}, f32[1,128,40]{1,2,0:T(8,128)}, u32[]{:S(2)}) copy-start(f32[1,128,40]{1,2,0:T(8,128)} %param.26) | copy-start | bytes 61444
  7.2 5.7 %copy-start.12 = (f32[40]{0:T(128)S(1)}, f32[40]{0:T(128)}, u32[]{:S(2)}) copy-start(f32[40]{0:T(128)} %param.29) | copy-start | bytes 484
  7.2 6.8 %copy-start.2 = (bf16[1,128,128]{2,1,0:T(8,128)(2,1)S(1)}, bf16[1,128,128]{2,1,0:T(8,128)(2,1)}, u32[]{:S(2)}) copy-start(bf16[1,128,128]{2,1,0:T(8,128)(2,1)} %param.28) | copy-start | bytes 98308
  7.2 248.7 %all-gather.8.cloned.1.call-start = ((), (), s32[]{:S(2)}) async-start(), calls=%async_computation.1 | async-start | bytes 11796480 | tf_op jit(solution)/shard_map/all_gather | solution.py:350
  14.0 238.2 %copy-start.3 = (f32[128,40]{0,1:T(8,128)}, f32[128,40]{0,1:T(8,128)S(1)}, u32[]{:S(2)}) copy-start(f32[128,40]{0,1:T(8,128)S(1)} %get-tuple-element.237) | copy-start | bytes 61444
  14.0 1.9 copy-start.5
  15.9 1.2 copy-start.8
  15.9 280.5 %all-gather.6.cloned.1.call-start = ((), (), s32[]{:S(2)}) async-start(), calls=%async_computation | async-start | bytes 11796480 | tf_op jit(solution)/shard_map/all_gather | solution.py:350
  256.0 0.7 copy-start.4
  256.0 0.7 copy-start.10
  256.1 0.6 copy-start.9
  296.6 16.2 %copy-start.1 = (f32[128,40,64]{0,2,1:T(8,128)S(1)}, f32[128,40,64]{0,2,1:T(8,128)}, u32[]{:S(2)}) copy-start(f32[128,40,64]{0,2,1:T(8,128)} %fusion.9) | copy-start | bytes 3932164
  296.6 16.2 %copy-start.6 = (f32[128,40]{0,1:T(8,128)S(1)}, f32[128,40]{0,1:T(8,128)}, u32[]{:S(2)}) copy-start(f32[128,40]{0,1:T(8,128)} %get-tuple-element.236) | copy-start | bytes 61444
  296.6 16.2 %copy-start.11 = (f32[40]{0:T(128)S(1)}, f32[40]{0:T(128)}, u32[]{:S(2)}) copy-start(f32[40]{0:T(128)} %param.30) | copy-start | bytes 484
Sparse Core Ops, SparseCore 0:
  16.0 105.4 all-gather.7
  236.9 59.4 all-gather.5

commit v2 on v0

v2 whole, which is shorter than its diff:
```python
import functools

import jax
import jax.numpy as jnp
from jax import lax
from jax.experimental import pallas as pl
from jax.experimental.pallas import tpu as pltpu
from jax.sharding import PartitionSpec as P

highest = lax.Precision.HIGHEST
MESH = pl.DeviceIdType.MESH
F32 = jnp.float32
BF16 = jnp.bfloat16

T = 128
D = 2560
E = 64
K = 8
FH = 256
NZ, NX, NY = 8, 4, 4
GR = D // 8
DR = FH // 8
HEADS = 40
N = 128
Q = D // 4
NEG = -1e30
SLOT = {4: 0, 3: 1, -3: 2, 2: 3, -2: 4, 1: 5, -1: 6, 0: 7}


def head_columns(first, count):
    h = lax.broadcasted_iota(jnp.int32, (N, count), 0)
    c = lax.broadcasted_iota(jnp.int32, (N, count), 1) + first
    return jnp.where((c >= h * 64) & (c < h * 64 + 64), 1.0, 0.0).astype(BF16)


def spread_heads(a, first, count):
    pick = head_columns(first, count)
    hi = a.astype(BF16)
    lo = (a - hi.astype(F32)).astype(BF16)
    return jnp.dot(hi, pick, preferred_element_type=F32) + jnp.dot(lo, pick, preferred_element_type=F32)


def kernel(
    x_hbm, router_ref, gu_hbm, dn_hbm, sgu_hbm, sdn_hbm, idx_ref, len_ref, raw_ref, b_ref, c_ref,
    rate_ref, skip_ref, cot_ref, out_ref, grad_ref,
    xall, gall, wg, wd, hid, part, shared, rr, rl, sr, sl_,
    cum, cumt, dt, dtt, aff, same, bt, ct, carried, closing, wmat, keeps, kown, ksib, skips, intra,
    lown, lsib, town, tin, sown, sin, lownb, lsibb, townb, tinb, sownb, sinb,
    loc, ss, rs,
):
    ctx = lax.axis_index("ctx")
    exp = lax.axis_index("exp")
    z, x = exp // NX, exp % NX
    y, core = ctx // 2, ctx % 2
    zp = {"exp": (exp + NX) % (NX * NZ)}
    zm = {"exp": (exp + NX * (NZ - 1)) % (NX * NZ)}
    xp = {"exp": z * NX + (x + 1) % NX}
    xm = {"exp": z * NX + (x + NX - 1) % NX}
    yp = {"ctx": (ctx + 2) % 8}
    ym = {"ctx": (ctx + 6) % 8}
    sib = {"ctx": ctx + 1 - 2 * core}
    y1, y2, y3 = (y + 1) % NY, (y + 2) % NY, (y + 3) % NY
    other = 1 - core

    counter = [0]

    def rcopy(src, dst, dev, k):
        return pltpu.make_async_remote_copy(
            src_ref=src, dst_ref=dst, send_sem=ss.at[k], recv_sem=rs.at[k],
            device_id=dev, device_id_type=MESH,
        )

    sent = []

    def send(src, dst, dev):
        k = counter[0]
        counter[0] += 1
        c = rcopy(src, dst, dev, k)
        c.start()
        sent.append(c)
        return k

    def arrived(k, region):
        rcopy(region, region, sib, k).wait_recv()

    barrier = pltpu.get_barrier_semaphore()
    for dev in (zp, zm, xp, xm, yp, ym, sib):
        pl.semaphore_signal(barrier, inc=1, device_id=dev, device_id_type=MESH)

    x_own = xall.at[SLOT[0]]
    lx = pltpu.make_async_copy(x_hbm.at[0], x_own, loc.at[0])
    lx.start()
    SG, SU, SD = 0, D, 2 * D
    shared_copies = [
        pltpu.make_async_copy(sgu_hbm.at[:, pl.ds(0, FH)], hid.at[pl.ds(SG, D)], loc.at[3]),
        pltpu.make_async_copy(sgu_hbm.at[:, pl.ds(FH, FH)], hid.at[pl.ds(SU, D)], loc.at[4]),
    ] + [
        pltpu.make_async_copy(
            sdn_hbm.at[:, pl.ds(i * FH, FH)], hid.at[pl.ds(SD + i * FH, FH)], loc.at[5 + i]
        )
        for i in range(D // FH)
    ]
    for c in shared_copies:
        c.start()
    pl.semaphore_wait(barrier, 7)

    kx = {}
    kx[-1] = send(x_hbm.at[0], xall.at[SLOT[-1]], zp)
    kx[1] = send(x_hbm.at[0], xall.at[SLOT[1]], zm)

    HC = D // 2
    parts = {"g": (gu_hbm, wg, GR, None), "d0": (dn_hbm, wd, DR, pl.ds(0, HC)), "d1": (dn_hbm, wd, DR, pl.ds(HC, HC))}

    def region(name, slot, e, yy, cc, rows=slice(None)):
        w, cols = parts[name][1], parts[name][3]
        return w.at[slot, e, yy, cc, rows] if cols is None else w.at[slot, e, yy, cc, rows, cols]

    def mine(name, e):
        w, cols = parts[name][0], parts[name][3]
        if e is None:
            return w if cols is None else w.at[:, :, cols]
        return w.at[e] if cols is None else w.at[e, :, cols]

    key = {}
    every = slice(None)

    def zeroth(name):
        key[name, "A", 2] = send(mine(name, 0), region(name, 2, 0, y, core), xp)
        key[name, "A", 1] = send(mine(name, 0), region(name, 1, 0, y, core), xm)
        key[name, "B", 3] = send(mine(name, 1), region(name, 0, 1, y, core), yp)
        key[name, "B", 1] = send(mine(name, 1), region(name, 0, 1, y, core), ym)
        key[name, "S"] = send(mine(name, None), region(name, 0, every, y, core), sib)

    def first_ring(name):
        h = parts[name][2] // 2
        lo_, hi_ = pl.ds(0, h), pl.ds(h, h)
        arrived(key[name, "A", 2], region(name, 2, 0, y, core))
        key[name, "hA", 2] = send(region(name, 2, 0, y, core, lo_), region(name, 3, 0, y, core, lo_), xp)
        arrived(key[name, "A", 1], region(name, 1, 0, y, core))
        key[name, "hA", 1] = send(region(name, 1, 0, y, core, hi_), region(name, 3, 0, y, core, hi_), xm)
        b3, b1 = region(name, 0, 1, y3, core), region(name, 0, 1, y1, core)
        arrived(key[name, "B", 3], b3)
        key[name, "hB", 3] = send(region(name, 0, 1, y3, core, lo_), region(name, 0, 1, y3, core, lo_), yp)
        arrived(key[name, "B", 1], b1)
        key[name, "hB", 1] = send(region(name, 0, 1, y1, core, hi_), region(name, 0, 1, y1, core, hi_), ym)
        key[name, "B3S"] = send(b3, b3, sib)
        key[name, "B1S"] = send(b1, b1, sib)

    def second_ring(name):
        h = parts[name][2] // 2
        lo_, hi_ = pl.ds(0, h), pl.ds(h, h)
        arrived(key[name, "hA", 2], region(name, 3, 0, y, core, lo_))
        arrived(key[name, "hA", 1], region(name, 3, 0, y, core, hi_))
        a = region(name, every, 0, y, core)
        key[name, "sA", 3] = send(a, a, yp)
        key[name, "sA", 1] = send(a, a, ym)
        arrived(key[name, "hB", 3], region(name, 0, 1, y2, core, lo_))
        arrived(key[name, "hB", 1], region(name, 0, 1, y2, core, hi_))
        b = region(name, 0, 1, every, core)
        key[name, "sB", 2] = send(b, region(name, 2, 1, every, core), xp)
        key[name, "sB", 1] = send(b, region(name, 1, 1, every, core), xm)
        s = region(name, 0, 1, y2, core)
        key[name, "B2S"] = send(s, s, sib)
        s = region(name, pl.ds(1, 3), 0, y, core)
        key[name, "AS"] = send(s, s, sib)

    def third(name):
        b2, b1 = region(name, 2, 1, every, core), region(name, 1, 1, every, core)
        arrived(key[name, "sB", 2], b2)
        two = pl.ds(0, 2)
        key[name, "lB", 2] = send(region(name, 2, 1, two, core), region(name, 3, 1, two, core), xp)
        arrived(key[name, "sB", 1], b1)
        two = pl.ds(2, 2)
        key[name, "lB", 1] = send(region(name, 1, 1, two, core), region(name, 3, 1, two, core), xm)
        a3, a1 = region(name, every, 0, y3, core), region(name, every, 0, y1, core)
        arrived(key[name, "sA", 3], a3)
        s = region(name, pl.ds(0, 2), 0, y3, core)
        key[name, "lA", 3] = send(s, s, yp)
        arrived(key[name, "sA", 1], a1)
        s = region(name, pl.ds(2, 2), 0, y1, core)
        key[name, "lA", 1] = send(s, s, ym)
        for k, s in (("tB2", b2), ("tB1", b1), ("tA3", a3), ("tA1", a1)):
            key[name, k] = send(s, s, sib)

    def fourth(name):
        arrived(key[name, "lA", 3], region(name, pl.ds(0, 2), 0, y2, core))
        arrived(key[name, "lA", 1], region(name, pl.ds(2, 2), 0, y2, core))
        s = region(name, every, 0, y2, core)
        key[name, "fA"] = send(s, s, sib)
        arrived(key[name, "lB", 2], region(name, 3, 1, pl.ds(0, 2), core))
        arrived(key[name, "lB", 1], region(name, 3, 1, pl.ds(2, 2), core))
        s = region(name, 3, 1, every, core)
        key[name, "fB"] = send(s, s, sib)

    def sibling_first(name):
        arrived(key[name, "S"], region(name, 0, every, y, other))
        arrived(key[name, "B3S"], region(name, 0, 1, y3, other))
        arrived(key[name, "B1S"], region(name, 0, 1, y1, other))
        arrived(key[name, "B2S"], region(name, 0, 1, y2, other))

    def sibling_third(name):
        arrived(key[name, "tB2"], region(name, 2, 1, every, other))
        arrived(key[name, "tB1"], region(name, 1, 1, every, other))

    def sibling_last(name):
        arrived(key[name, "AS"], region(name, pl.ds(1, 3), 0, y, other))
        arrived(key[name, "tA3"], region(name, every, 0, y3, other))
        arrived(key[name, "tA1"], region(name, every, 0, y1, other))
        arrived(key[name, "fA"], region(name, every, 0, y2, other))
        arrived(key[name, "fB"], region(name, 3, 1, every, other))

    for name in ("g", "d0", "d1"):
        zeroth(name)
    lg = pltpu.make_async_copy(gu_hbm, wg.at[0, :, y, core], loc.at[1])
    ld = pltpu.make_async_copy(dn_hbm, wd.at[0, :, y, core], loc.at[2])
    lg.start()
    ld.start()

    lx.wait()
    xo = x_own[...]
    logits = jnp.dot(xo, router_ref[...], preferred_element_type=F32)
    lane = lax.broadcasted_iota(jnp.int32, (T, E), 1)
    chosen = jnp.zeros((T, E), F32)
    idx = idx_ref[0]
    for j in range(K):
        chosen = chosen + jnp.where(idx[:, j : j + 1] == lane, 1.0, 0.0)
    sig = chosen * jax.nn.sigmoid(logits)
    gate = sig / jnp.sum(sig, axis=1, keepdims=True)
    hi = gate.astype(BF16)
    lo = (gate - hi.astype(F32)).astype(BF16)
    gall[SLOT[0], :, 0:E] = hi
    gall[SLOT[0], :, E : 2 * E] = lo
    kg = {}
    kg[-1] = send(gall.at[SLOT[0]], gall.at[SLOT[-1]], zp)
    kg[1] = send(gall.at[SLOT[0]], gall.at[SLOT[1]], zm)

    def shared_expert():
        for c in shared_copies:
            c.wait()
        xo = x_own[...]
        sa = jnp.dot(xo, hid[SG : SG + D], preferred_element_type=F32)
        sb = jnp.dot(xo, hid[SU : SU + D], preferred_element_type=F32)
        sh = (jax.nn.silu(sa) * sb).astype(BF16)
        for i in range(D // FH):
            cols = slice(i * FH, (i + 1) * FH)
            shared[:, cols] = xo[:, cols].astype(F32) + jnp.dot(
                sh, hid[SD + i * FH : SD + (i + 1) * FH], preferred_element_type=F32
            )

    def token_step(d):
        for buf, keys in ((xall, kx), (gall, kg)):
            arrived(keys[-d], buf.at[SLOT[-d]])
            arrived(keys[d], buf.at[SLOT[d]])
            if d < 3:
                keys[-d - 1] = send(buf.at[SLOT[-d]], buf.at[SLOT[-d - 1]], zp)
                keys[d + 1] = send(buf.at[SLOT[d]], buf.at[SLOT[d + 1]], zm)
            else:
                lo_, hi_ = pl.ds(0, T // 2), pl.ds(T // 2, T // 2)
                keys["lo"] = send(buf.at[SLOT[-3], lo_], buf.at[SLOT[4], lo_], zp)
                keys["hi"] = send(buf.at[SLOT[3], hi_], buf.at[SLOT[4], hi_], zm)

    row_i = lax.broadcasted_iota(jnp.int32, (T, T), 0)
    col_i = lax.broadcasted_iota(jnp.int32, (T, T), 1)
    second_f = core == 1
    second_b = core == 0

    def decays():
        dt[...] = jnp.zeros((T, N), F32)
        cum[...] = jnp.zeros((T, N), F32)
        steps = jax.nn.softplus(raw_ref[0])
        dt[:, 0:HEADS] = steps
        cum[:, 0:HEADS] = -steps * rate_ref[...]
        lower = jnp.where(row_i >= col_i, 1.0, 0.0)
        c = jnp.dot(lower, cum[...], precision=highest, preferred_element_type=F32)
        cum[...] = c
        cumt[...] = c.T
        dtt[...] = dt[...].T
        b, cc = b_ref[0], c_ref[0]
        bt[...] = b.astype(F32).T.astype(BF16)
        ct[...] = cc.astype(F32).T.astype(BF16)
        lens = jnp.broadcast_to(len_ref[...].astype(F32), (8, 8))
        before = lax.broadcasted_iota(jnp.int32, (8, 8), 1) < lax.broadcasted_iota(jnp.int32, (8, 8), 0)
        starts = jnp.sum(jnp.where(before, lens, 0.0), axis=1, keepdims=True)
        offset = (ctx * T).astype(F32)
        place = lax.broadcasted_iota(jnp.int32, (8, T), 1).astype(F32) + offset

        def number(p):
            return jnp.sum(jnp.where(starts <= p, 1.0, 0.0), axis=0, keepdims=True)

        doc_row = jnp.broadcast_to(number(place), (T, T))
        doc_col = doc_row.T
        ahead = jnp.broadcast_to(number(place[:, 0:1] - 1.0), (T, T))
        final = jnp.broadcast_to(number(place[:, T - 1 : T]), (T, T))
        same[...] = jnp.where(doc_row == doc_col, 1.0, 0.0)
        end = c[T - 1 : T, :]
        carry = jnp.exp(c) * jnp.where(doc_col == ahead, 1.0, 0.0)
        close = jnp.exp(end - c) * jnp.where(doc_col == final, 1.0, 0.0) * dt[...]
        keep = jnp.exp(end) * jnp.where(final[0:1] == ahead[0:1], 1.0, 0.0)
        keeps[0] = jnp.broadcast_to(keep, (8, N))
        key["keep"] = send(keeps.at[0], keeps.at[1], sib)
        skip = jnp.concatenate([skip_ref[...], jnp.zeros((1, N - HEADS), F32)], axis=1)
        for i in range(4):
            cols = slice(i * Q, (i + 1) * Q)
            carried[:, cols] = spread_heads(carry, i * Q, Q)
            closing[:, cols] = spread_heads(close, i * Q, Q)
            skips[:, cols] = spread_heads(jnp.broadcast_to(skip, (8, N)), i * Q, Q)
            kown[:, cols] = spread_heads(keeps[0], i * Q, Q)
        aff[...] = lax.dot_general(cc, b, (((1,), (1,)), ((), ())), preferred_element_type=F32)

    def column(a, h):
        return jnp.sum(jnp.where(col_i == h, a, 0.0), axis=1, keepdims=True)

    def forward_weights():
        causal = (same[...] > 0.5) & (row_i >= col_i)
        a = aff[...]
        c = cum[...]

        def pair(p, _):
            for j in range(2):
                h = 2 * p + j
                gap = column(c, h) - cumt[pl.ds(h, 1), :]
                w = a * jnp.exp(jnp.where(causal, gap, NEG)) * dtt[pl.ds(h, 1), :]
                wmat[p, j * T : (j + 1) * T, :] = w.astype(BF16)
            return 0

        lax.fori_loop(0, HEADS // 2, pair, 0)

    def gradient_states():
        for i in range(4):
            cols = slice(i * Q, (i + 1) * Q)
            v = (carried[:, cols] * cot_ref[0, :, cols].astype(F32)).astype(BF16)
            lownb[:, cols] = jnp.dot(ct[...], v, preferred_element_type=F32).astype(BF16)
        key["lb"] = send(lownb, lsibb, sib)
        arrived(key["keep"], keeps.at[1])
        for i in range(4):
            cols = slice(i * Q, (i + 1) * Q)
            ksib[:, cols] = spread_heads(keeps[1], i * Q, Q)

    rows_own = pl.ds(pl.multiple_of(core * 64, 64), 64)
    rows_other = pl.ds(pl.multiple_of(other * 64, 64), 64)

    def chip_state(cols, lo_, ls, to, second):
        ko, ks = kown[0:1, cols], ksib[0:1, cols]
        one = jnp.ones_like(ko)
        t = jnp.where(second, one, ks) * lo_[rows_own, cols].astype(F32)
        t = t + jnp.where(second, ko, one) * ls[rows_own, cols].astype(F32)
        to[:, cols] = t.astype(BF16)

    def passed_on(cols, to, ti, so):
        k = kown[0:1, cols] * ksib[0:1, cols]
        so[:, cols] = (to[:, cols].astype(F32) + k * ti[:, cols].astype(F32)).astype(BF16)

    def entering(cols, ls, si, second):
        ks = ksib[0:1, cols]
        s = jnp.where(second, ks, jnp.ones_like(ks)) * si[:, cols].astype(F32)
        s = s + jnp.where(second, 1.0, 0.0) * ls[:, cols].astype(F32)
        return s.astype(BF16)

    def gradient_one():
        arrived(key["lb"], lsibb)
        for i in range(4):
            chip_state(slice(i * Q, (i + 1) * Q), lownb, lsibb, townb, second_b)
        key["tb"] = send(townb, tinb, ym)

    def gradient_two():
        arrived(key["tb"], tinb)
        for i in range(4):
            passed_on(slice(i * Q, (i + 1) * Q), townb, tinb, sownb)
        key["sb"] = send(sownb, sinb.at[rows_own], ym)

    def gradient_three():
        arrived(key["sb"], sinb.at[rows_own])
        key["ob"] = send(sinb.at[rows_own], sinb.at[rows_own], sib)

    def gradient_four():
        arrived(key["ob"], sinb.at[rows_other])
        causal = (same[...] > 0.5) & (row_i <= col_i)
        b = b_ref[0]
        a = lax.dot_general(b, c_ref[0], (((1,), (1,)), ((), ())), preferred_element_type=F32)
        c = cum[...]
        d = dt[...]
        left = col_i < 64

        def pair(p, _):
            cols = pl.ds(pl.multiple_of(p * N, N), N)
            seed = cot_ref[0, :, cols]
            halves = []
            for j in range(2):
                h = 2 * p + j
                gap = cumt[pl.ds(h, 1), :] - column(c, h)
                w = a * jnp.exp(jnp.where(causal, gap, NEG)) * column(d, h)
                halves.append(jnp.dot(w.astype(BF16), seed, preferred_element_type=F32))
            g = jnp.where(left, halves[0], halves[1])
            s = entering(cols, lsibb, sinb, second_b)
            g = g + closing[:, cols] * jnp.dot(b, s, preferred_element_type=F32)
            g = g + skips[0:1, cols] * seed.astype(F32)
            grad_ref[0, :, cols] = g.astype(BF16)
            return 0

        lax.fori_loop(0, HEADS // 2, pair, 0)

    def forward_zero(q, u):
        cols = slice(q * Q, (q + 1) * Q)
        v = (closing[:, cols] * u.astype(F32)).astype(BF16)
        lown[:, cols] = jnp.dot(bt[...], v, preferred_element_type=F32).astype(BF16)
        key["l", q] = send(lown.at[:, cols], lsib.at[:, cols], sib)
        left = col_i < 64
        for i in range(Q // N):
            p = q * (Q // N) + i
            pc = slice(p * N, (p + 1) * N)
            up = u[:, i * N : (i + 1) * N]
            r = jnp.dot(wmat[p], up, preferred_element_type=F32)
            intra[:, pc] = jnp.where(left, r[0:T], r[T:]) + skips[0:1, pc] * up.astype(F32)

    def forward_one(q):
        cols = slice(q * Q, (q + 1) * Q)
        arrived(key["l", q], lsib.at[:, cols])
        chip_state(cols, lown, lsib, town, second_f)
        key["t", q] = send(town.at[:, cols], tin.at[:, cols], yp)

    def forward_two(q):
        cols = slice(q * Q, (q + 1) * Q)
        arrived(key["t", q], tin.at[:, cols])
        passed_on(cols, town, tin, sown)
        key["s", q] = send(sown.at[:, cols], sin.at[rows_own, cols], yp)

    def forward_three(q):
        cols = slice(q * Q, (q + 1) * Q)
        arrived(key["s", q], sin.at[rows_own, cols])
        key["o", q] = send(sin.at[rows_own, cols], sin.at[rows_own, cols], sib)

    def forward_four(q):
        cols = slice(q * Q, (q + 1) * Q)
        arrived(key["o", q], sin.at[rows_other, cols])
        s = entering(cols, lsib, sin, second_f)
        r = intra[:, cols] + carried[:, cols] * jnp.dot(c_ref[0], s, preferred_element_type=F32)
        out_ref[0, :, cols] = r.astype(BF16)

    MT = 256

    def hidden_tile(n, m):
        slot, e = n // 2, n % 2
        away = jnp.where(slot == 2, 3, jnp.where(slot == 3, 2, slot))
        expert = 2 * (z * NX + (x + away) % NX) + e
        r = lax.broadcasted_iota(jnp.int32, (2 * E, FH), 0)
        sel = jnp.where((r == expert) | (r == expert + E), 1.0, 0.0).astype(BF16)
        xs = xall[pl.ds(m * (MT // T), MT // T)].reshape(MT, D)
        gs = gall[pl.ds(m * (MT // T), MT // T)].reshape(MT, 2 * E)
        w = wg[slot, e].reshape(D, 2 * FH)
        p = jnp.dot(xs, w, preferred_element_type=F32)
        g = jnp.dot(gs, sel, preferred_element_type=F32)
        h = (jax.nn.silu(p[:, :FH]) * p[:, FH:] * g).astype(BF16)
        hid[pl.ds(pl.multiple_of(n * NZ * T + m * MT, MT), MT), :] = h

    def hidden(experts, tiles):
        def one(i, _):
            hidden_tile(experts[0] + experts[1] * (i // tiles[1]), tiles[0] + i % tiles[1])
            return 0

        lax.fori_loop(0, experts[2] * tiles[1], one, 0)

    NC = 256

    def partial(first, rows, hf, into):
        def tile(c, _):
            cols = pl.ds(pl.multiple_of(hf * HC + c * NC, NC), NC)
            acc = jnp.zeros((rows, NC), F32)
            for n in range(8):
                acc = acc + jnp.dot(
                    hid[pl.ds(n * NZ * T + first * T, rows), :],
                    wd[n // 2, n % 2, :, :, :, cols].reshape(FH, NC),
                    preferred_element_type=F32,
                )
            if into is part:
                part[pl.ds(0, rows), pl.ds(pl.multiple_of(c * NC, NC), NC)] = acc
            else:
                into[:, cols] += acc
            return 0

        lax.fori_loop(0, HC // NC, tile, 0)

    kr, kl = {}, {}
    c0, c1 = slice(0, Q), slice(Q, 2 * Q)

    def scatter_start(hf):
        partial(SLOT[4], T, hf, part)
        sr[hf, 0] = part[0:T, c0].astype(BF16)
        kr[hf, 0] = send(sr.at[hf, 0], rr.at[hf, 0], zp)
        sl_[hf, 0] = part[0:T, c1].astype(BF16)
        kl[hf, 0] = send(sl_.at[hf, 0], rl.at[hf, 0], zm)
        partial(SLOT[3], 2 * T, hf, part)
        sr[hf, 1] = part[0:T, c1].astype(BF16)
        kr[hf, 1] = send(sr.at[hf, 1], rr.at[hf, 1], zp)
        sl_[hf, 1] = part[T : 2 * T, c0].astype(BF16)
        kl[hf, 1] = send(sl_.at[hf, 1], rl.at[hf, 1], zm)

    def relay(hf, k):
        cr, cl = (c0, c1) if k % 2 == 0 else (c1, c0)
        arrived(kr[hf, k], rr.at[hf, k])
        rr[hf, k] = (rr[hf, k].astype(F32) + part[0:T, cr]).astype(BF16)
        kr[hf, k + 2] = send(rr.at[hf, k], rr.at[hf, k + 2], zp)
        arrived(kl[hf, k], rl.at[hf, k])
        rl[hf, k] = (rl[hf, k].astype(F32) + part[T : 2 * T, cl]).astype(BF16)
        kl[hf, k + 2] = send(rl.at[hf, k], rl.at[hf, k + 2], zm)

    def mixer_in(hf):
        for k in (5, 6):
            arrived(kr[hf, k], rr.at[hf, k])
            arrived(kl[hf, k], rl.at[hf, k])
        for i, (a, b) in enumerate(((6, 5), (5, 6))):
            q = 2 * hf + i
            cols = slice(q * Q, (q + 1) * Q)
            u = shared[:, cols] + rr[hf, a].astype(F32) + rl[hf, b].astype(F32)
            forward_zero(q, u.astype(BF16))

    shared_expert()
    decays()
    gradient_states()
    lg.wait()
    ld.wait()
    first_ring("g")
    second_ring("g")
    token_step(1)
    first_ring("d0")
    first_ring("d1")
    forward_weights()
    sibling_first("g")
    hidden((1, 2, 1), (3, 1))
    token_step(2)
    hidden((1, 2, 1), (2, 1))
    third("g")
    token_step(3)
    second_ring("d0")
    second_ring("d1")
    sibling_third("g")
    hidden((3, 2, 2), (2, 2))
    hidden((1, 2, 3), (1, 1))
    for buf, keys in ((xall, kx), (gall, kg)):
        arrived(keys["lo"], buf.at[SLOT[4], pl.ds(0, T // 2)])
        arrived(keys["hi"], buf.at[SLOT[4], pl.ds(T // 2, T // 2)])
    fourth("g")
    hidden((1, 2, 3), (0, 1))
    sibling_last("g")
    hidden((0, 2, 2), (0, 4))
    third("d0")
    hidden((4, 2, 2), (0, 4))
    hidden((7, 2, 1), (0, 4))
    third("d1")
    fourth("d0")
    sibling_first("d0")
    sibling_third("d0")
    sibling_last("d0")
    scatter_start(0)
    relay(0, 0)
    partial(SLOT[2], 2 * T, 0, part)
    fourth("d1")
    relay(0, 1)
    relay(0, 2)
    partial(SLOT[1], 2 * T, 0, part)
    relay(0, 3)
    relay(0, 4)
    sibling_first("d1")
    sibling_third("d1")
    sibling_last("d1")
    scatter_start(1)
    partial(SLOT[0], T, 0, shared)
    mixer_in(0)
    relay(1, 0)
    partial(SLOT[2], 2 * T, 1, part)
    gradient_one()
    forward_one(0)
    forward_one(1)
    relay(1, 1)
    relay(1, 2)
    partial(SLOT[1], 2 * T, 1, part)
    gradient_two()
    forward_two(0)
    forward_two(1)
    relay(1, 3)
    relay(1, 4)
    partial(SLOT[0], T, 1, shared)
    forward_three(0)
    forward_three(1)
    gradient_three()
    gradient_four()
    forward_four(0)
    forward_four(1)
    mixer_in(1)
    for stage in (forward_one, forward_two, forward_three, forward_four):
        stage(2)
        stage(3)
    for c in sent:
        c.wait_send()


COPIES = 2 + 3 * 27 + 2 + 12 + 28 + 1 + 4 + 16


def on_device(
    tokens, router, gate_up, down, shared_gate_up, shared_down, routes, lengths,
    steps, writes, reads, decay_rate, skip_gain, cotangent,
):
    vmem = pl.BlockSpec(memory_space=pltpu.VMEM)
    hbm = pl.BlockSpec(memory_space=pl.ANY)
    wide = pltpu.VMEM((T, D), F32)
    square = pltpu.VMEM((T, N), F32)
    small = pltpu.VMEM((N, N), BF16)
    state = pltpu.VMEM((N, D), BF16)
    half = pltpu.VMEM((N // 2, D), BF16)
    row = pltpu.VMEM((8, D), F32)
    return pl.pallas_call(
        kernel,
        out_shape=[jax.ShapeDtypeStruct((1, T, D), BF16)] * 2,
        in_specs=[hbm, vmem, hbm, hbm, hbm, hbm] + [vmem] * 8,
        out_specs=[vmem, vmem],
        scratch_shapes=[
            pltpu.VMEM((NZ, T, D), BF16),
            pltpu.VMEM((NZ, T, 2 * E), BF16),
            pltpu.VMEM((NX, 2, NY, 2, GR, 2 * FH), BF16),
            pltpu.VMEM((NX, 2, NY, 2, DR, D), BF16),
            pltpu.VMEM((NX * 2 * NZ * T, FH), BF16),
            pltpu.VMEM((2 * T, 2 * Q), F32),
            wide,
            pltpu.VMEM((2, 7, T, Q), BF16),
            pltpu.VMEM((2, 7, T, Q), BF16),
            pltpu.VMEM((2, 2, T, Q), BF16),
            pltpu.VMEM((2, 2, T, Q), BF16),
            square, square, square, square, square, square, small, small, wide, wide,
            pltpu.VMEM((HEADS // 2, 2 * T, T), BF16),
            pltpu.VMEM((2, 8, N), F32),
            row, row, row, wide,
            state, state, half, half, half, state,
            state, state, half, half, half, state,
            pltpu.SemaphoreType.DMA((5 + D // FH,)),
            pltpu.SemaphoreType.DMA((COPIES,)),
            pltpu.SemaphoreType.DMA((COPIES,)),
        ],
        compiler_params=pltpu.CompilerParams(
            collective_id=0, has_side_effects=True, vmem_limit_bytes=63 * 2**20
        ),
    )(
        tokens, router, gate_up, down, shared_gate_up, shared_down, routes, lengths,
        steps, writes, reads, decay_rate.reshape(1, -1), skip_gain.reshape(1, -1), cotangent,
    )


def solution(mesh):
    return jax.shard_map(
        on_device,
        mesh=mesh,
        in_specs=(
            P("exp", "ctx", None),
            P(),
            P("exp", "ctx", None),
            P("exp", "ctx", None),
            P(),
            P(),
            P("exp", "ctx", None),
            P("exp", None),
            P("exp", "ctx", None),
            P("exp", "ctx", None),
            P("exp", "ctx", None),
            P(),
            P(),
            P("exp", "ctx", None),
        ),
        out_specs=(P("exp", "ctx", None), P("exp", "ctx", None)),
        check_vma=False,
    )
```

time: 576 us -> 185 us (0.32)
  the two profiles are of different devices: /device:TPU:27 before, /device:TPU:1 now
where the time goes in v2:
time: 185 us
  Pallas kernels  176 us (95%)
  local copies, waits for them, and re-layouts  8.84 us (5%)
    pallas_call x1, Pallas kernels, on_device(): pl.pallas_call(kernel, out_shape=[jax.ShapeDtypeStruct((1, T, D), BF16)]...  176 us
    unnamed x5, local copies, waits for them, and re-layouts  8.84 us

profile of v2, /device:TPU:1, one launch (start us, length us, event | category | flops | bytes accessed | tf_op | source)
XLA Modules:
  0.0 185.1 jit_solution(6702460645394973296)
XLA Ops:
  0.6 1.4 copy.17.idx_ref
  2.0 1.4 copy.18.raw_ref
  3.5 2.1 %copy.16.router_ref = bf16[2560,64]{1,0:T(8,128)(2,1)} copy(bf16[2560,64]{0,1:T(8,128)(2,1)} %param.15) | data formatting | bytes 655360 | tf_op args[1]
  5.5 175.6 %shard_map.149 = (bf16[1,128,2560]{2,1,0:T(8,128)(2,1)}, bf16[1,128,2560]{2,1,0:T(8,128)(2,1)}) custom-call(bf16[1,128,2560]{2,1,0:T(8,128)(2,1)} %x_hbm.1, bf16[2560,64]{1,0:T(8,128)(2,1)} %copy.16.router_ref, bf16[2,320,512]{2,1,0:T(8,128)(2,1)} %gu_hbm.1, bf16[2,32,2560]{2,1,0:T(8,128)(2,1)} %dn_hbm.1, bf16[2560,512]{1,0:T(8,128)(2,1)} %sgu_hbm.1, ...), custom_call_target="tpu_custom_call" | custom-call | tf_op jit(solution)/shard_map/pallas_call | solution.py:611
  181.2 2.0 %copy.21 = bf16[1,128,2560]{2,1,0:T(8,128)(2,1)} copy(bf16[1,128,2560]{2,1,0:T(8,128)(2,1)} %get-tuple-element.4) | data formatting | bytes 1310720
  183.1 2.0 %copy.22 = bf16[1,128,2560]{2,1,0:T(8,128)(2,1)} copy(bf16[1,128,2560]{2,1,0:T(8,128)(2,1)} %get-tuple-element.5) | data formatting | bytes 1310720

commit v3 on v2

--- a/solution.py
+++ b/solution.py
@@ -129,7 +129,8 @@
         key[name, "A", 1] = send(mine(name, 0), region(name, 1, 0, y, core), xm)
         key[name, "B", 3] = send(mine(name, 1), region(name, 0, 1, y, core), yp)
         key[name, "B", 1] = send(mine(name, 1), region(name, 0, 1, y, core), ym)
-        key[name, "S"] = send(mine(name, None), region(name, 0, every, y, core), sib)
+        own = 1 if name == "g" else None
+        key[name, "S"] = send(mine(name, own), region(name, 0, every if own is None else own, y, core), sib)
 
     def first_ring(name):
         h = parts[name][2] // 2
@@ -146,7 +147,7 @@
         key[name, "B3S"] = send(b3, b3, sib)
         key[name, "B1S"] = send(b1, b1, sib)
 
-    def second_ring(name):
+    def second_ring_a(name):
         h = parts[name][2] // 2
         lo_, hi_ = pl.ds(0, h), pl.ds(h, h)
         arrived(key[name, "hA", 2], region(name, 3, 0, y, core, lo_))
@@ -154,6 +155,12 @@
         a = region(name, every, 0, y, core)
         key[name, "sA", 3] = send(a, a, yp)
         key[name, "sA", 1] = send(a, a, ym)
+        s = region(name, pl.ds(1, 3), 0, y, core)
+        key[name, "AS"] = send(s, s, sib)
+
+    def second_ring_b(name):
+        h = parts[name][2] // 2
+        lo_, hi_ = pl.ds(0, h), pl.ds(h, h)
         arrived(key[name, "hB", 3], region(name, 0, 1, y2, core, lo_))
         arrived(key[name, "hB", 1], region(name, 0, 1, y2, core, hi_))
         b = region(name, 0, 1, every, core)
@@ -161,8 +168,70 @@
         key[name, "sB", 1] = send(b, region(name, 1, 1, every, core), xm)
         s = region(name, 0, 1, y2, core)
         key[name, "B2S"] = send(s, s, sib)
-        s = region(name, pl.ds(1, 3), 0, y, core)
-        key[name, "AS"] = send(s, s, sib)
+
+    half_g = (pl.ds(0, GR // 2), pl.ds(GR // 2, GR // 2))
+
+    def slot_out(s):
+        a = region("g", s, 0, y, core)
+        key["sA", s, 3] = send(a, a, yp)
+        key["sA", s, 1] = send(a, a, ym)
+
+    def slot_on(s):
+        b3, b1 = region("g", s, 0, y3, core), region("g", s, 0, y1, core)
+        arrived(key["sA", s, 3], b3)
+        r = region("g", s, 0, y3, core, half_g[0])
+        key["lA", s, 3] = send(r, r, yp)
+        arrived(key["sA", s, 1], b1)
+        r = region("g", s, 0, y1, core, half_g[1])
+        key["lA", s, 1] = send(r, r, ym)
+        if s == 3:
+            for k, r in (("3y", region("g", 3, 0, y, core)), ("3y3", b3), ("3y1", b1)):
+                key["sib", k] = send(r, r, sib)
+
+    def slot_last(s):
+        arrived(key["lA", s, 3], region("g", s, 0, y2, core, half_g[0]))
+        arrived(key["lA", s, 1], region("g", s, 0, y2, core, half_g[1]))
+        r = region("g", s, 0, y2 if s == 3 else every, core)
+        key["sib", s] = send(r, r, sib)
+
+    def slot_sibling(s):
+        arrived(key["sib", s], region("g", s, 0, y2 if s == 3 else every, other))
+        if s == 3:
+            for k, yy in (("3y", y), ("3y3", y3), ("3y1", y1)):
+                arrived(key["sib", k], region("g", 3, 0, yy, other))
+
+    def second_ring_g():
+        arrived(key["g", "hA", 2], region("g", 3, 0, y, core, half_g[0]))
+        arrived(key["g", "hA", 1], region("g", 3, 0, y, core, half_g[1]))
+        slot_out(3)
+        arrived(key["g", "hB", 3], region("g", 0, 1, y2, core, half_g[0]))
+        arrived(key["g", "hB", 1], region("g", 0, 1, y2, core, half_g[1]))
+        b = region("g", 0, 1, every, core)
+        key["g", "sB", 2] = send(b, region("g", 2, 1, every, core), xp)
+        key["g", "sB", 1] = send(b, region("g", 1, 1, every, core), xm)
+        s = region("g", 0, 1, y2, core)
+        key["g", "B2S"] = send(s, s, sib)
+
+    def third_g():
+        b2, b1 = region("g", 2, 1, every, core), region("g", 1, 1, every, core)
+        arrived(key["g", "sB", 2], b2)
+        two = pl.ds(0, 2)
+        key["g", "lB", 2] = send(region("g", 2, 1, two, core), region("g", 3, 1, two, core), xp)
+        arrived(key["g", "sB", 1], b1)
+        two = pl.ds(2, 2)
+        key["g", "lB", 1] = send(region("g", 1, 1, two, core), region("g", 3, 1, two, core), xm)
+        for k, s in (("tB2", b2), ("tB1", b1)):
+            key["g", k] = send(s, s, sib)
+
+    def fourth_g():
+        for k, two, cc in ((2, pl.ds(0, 2), 0), (1, pl.ds(2, 2), 1)):
+            s = region("g", 3, 1, two, core)
+            arrived(key["g", "lB", k], s)
+            key["g", "fB", k] = send(s, s, sib)
+
+    def sibling_fourth_g():
+        for k, two in ((2, pl.ds(0, 2)), (1, pl.ds(2, 2))):
+            arrived(key["g", "fB", k], region("g", 3, 1, two, other))
 
     def third(name):
         b2, b1 = region(name, 2, 1, every, core), region(name, 1, 1, every, core)
@@ -193,7 +262,7 @@
         key[name, "fB"] = send(s, s, sib)
 
     def sibling_first(name):
-        arrived(key[name, "S"], region(name, 0, every, y, other))
+        arrived(key[name, "S"], region(name, 0, 1 if name == "g" else every, y, other))
         arrived(key[name, "B3S"], region(name, 0, 1, y3, other))
         arrived(key[name, "B1S"], region(name, 0, 1, y1, other))
         arrived(key[name, "B2S"], region(name, 0, 1, y2, other))
@@ -209,8 +278,8 @@
         arrived(key[name, "fA"], region(name, every, 0, y2, other))
         arrived(key[name, "fB"], region(name, 3, 1, every, other))
 
-    for name in ("g", "d0", "d1"):
-        zeroth(name)
+    zeroth("g")
+    zeroth("d0")
     lg = pltpu.make_async_copy(gu_hbm, wg.at[0, :, y, core], loc.at[1])
     ld = pltpu.make_async_copy(dn_hbm, wd.at[0, :, y, core], loc.at[2])
     lg.start()
@@ -218,18 +287,18 @@
 
     lx.wait()
     xo = x_own[...]
-    logits = jnp.dot(xo, router_ref[...], preferred_element_type=F32)
-    lane = lax.broadcasted_iota(jnp.int32, (T, E), 1)
-    chosen = jnp.zeros((T, E), F32)
+    logits = lax.dot_general(
+        router_ref[...], xo, (((1,), (1,)), ((), ())), preferred_element_type=F32
+    )
+    number_of = lax.broadcasted_iota(jnp.int32, (E, T), 0)
+    chosen = jnp.zeros((E, T), F32)
     idx = idx_ref[0]
     for j in range(K):
-        chosen = chosen + jnp.where(idx[:, j : j + 1] == lane, 1.0, 0.0)
+        chosen = chosen + jnp.where(idx[j : j + 1, :] == number_of, 1.0, 0.0)
     sig = chosen * jax.nn.sigmoid(logits)
-    gate = sig / jnp.sum(sig, axis=1, keepdims=True)
-    hi = gate.astype(BF16)
-    lo = (gate - hi.astype(F32)).astype(BF16)
-    gall[SLOT[0], :, 0:E] = hi
-    gall[SLOT[0], :, E : 2 * E] = lo
+    gate = sig / jnp.sum(sig, axis=0, keepdims=True)
+    hi = gate.astype(BF16).astype(F32)
+    gall[SLOT[0]] = jnp.concatenate([hi, gate - hi], axis=0).T.astype(BF16)
     kg = {}
     kg[-1] = send(gall.at[SLOT[0]], gall.at[SLOT[-1]], zp)
     kg[1] = send(gall.at[SLOT[0]], gall.at[SLOT[1]], zm)
@@ -265,16 +334,15 @@
     second_b = core == 0
 
     def decays():
-        dt[...] = jnp.zeros((T, N), F32)
-        cum[...] = jnp.zeros((T, N), F32)
-        steps = jax.nn.softplus(raw_ref[0])
-        dt[:, 0:HEADS] = steps
-        cum[:, 0:HEADS] = -steps * rate_ref[...]
+        dtt[...] = jnp.zeros((N, T), F32)
+        dtt[0:HEADS, :] = jax.nn.softplus(raw_ref[0])
+        steps = dtt[...].T
+        dt[...] = steps
+        rate = jnp.concatenate([rate_ref[...], jnp.zeros((1, N - HEADS), F32)], axis=1)
         lower = jnp.where(row_i >= col_i, 1.0, 0.0)
-        c = jnp.dot(lower, cum[...], precision=highest, preferred_element_type=F32)
+        c = jnp.dot(lower, -steps * rate, precision=highest, preferred_element_type=F32)
         cum[...] = c
         cumt[...] = c.T
-        dtt[...] = dt[...].T
         b, cc = b_ref[0], c_ref[0]
         bt[...] = b.astype(F32).T.astype(BF16)
         ct[...] = cc.astype(F32).T.astype(BF16)
@@ -436,9 +504,7 @@
         r = intra[:, cols] + carried[:, cols] * jnp.dot(c_ref[0], s, preferred_element_type=F32)
         out_ref[0, :, cols] = r.astype(BF16)
 
-    MT = 256
-
-    def hidden_tile(n, m):
+    def hidden_tile(n, m, MT):
         slot, e = n // 2, n % 2
         away = jnp.where(slot == 2, 3, jnp.where(slot == 3, 2, slot))
         expert = 2 * (z * NX + (x + away) % NX) + e
@@ -452,32 +518,21 @@
         h = (jax.nn.silu(p[:, :FH]) * p[:, FH:] * g).astype(BF16)
         hid[pl.ds(pl.multiple_of(n * NZ * T + m * MT, MT), MT), :] = h
 
-    def hidden(experts, tiles):
+    def hidden(experts, tiles, rows=256):
         def one(i, _):
-            hidden_tile(experts[0] + experts[1] * (i // tiles[1]), tiles[0] + i % tiles[1])
+            hidden_tile(experts[0] + experts[1] * (i // tiles[1]), tiles[0] + i % tiles[1], rows)
             return 0
 
         lax.fori_loop(0, experts[2] * tiles[1], one, 0)
 
-    NC = 256
-
     def partial(first, rows, hf, into):
-        def tile(c, _):
-            cols = pl.ds(pl.multiple_of(hf * HC + c * NC, NC), NC)
-            acc = jnp.zeros((rows, NC), F32)
-            for n in range(8):
-                acc = acc + jnp.dot(
-                    hid[pl.ds(n * NZ * T + first * T, rows), :],
-                    wd[n // 2, n % 2, :, :, :, cols].reshape(FH, NC),
-                    preferred_element_type=F32,
-                )
-            if into is part:
-                part[pl.ds(0, rows), pl.ds(pl.multiple_of(c * NC, NC), NC)] = acc
-            else:
-                into[:, cols] += acc
-            return 0
-
-        lax.fori_loop(0, HC // NC, tile, 0)
+        h = jnp.concatenate([hid[pl.ds(n * NZ * T + first * T, rows), :] for n in range(8)], axis=1)
+        w = wd[:, :, :, :, :, hf * HC : (hf + 1) * HC].reshape(8 * FH, HC)
+        acc = jnp.dot(h, w, preferred_element_type=F32)
+        if into is part:
+            part[0:rows, :] = acc
+        else:
+            into[:, hf * HC : (hf + 1) * HC] += acc
 
     kr, kl = {}, {}
     c0, c1 = slice(0, Q), slice(Q, 2 * Q)
@@ -513,40 +568,59 @@
             u = shared[:, cols] + rr[hf, a].astype(F32) + rl[hf, b].astype(F32)
             forward_zero(q, u.astype(BF16))
 
-    shared_expert()
-    decays()
-    gradient_states()
     lg.wait()
     ld.wait()
+    shared_expert()
     first_ring("g")
-    second_ring("g")
+    for slot in range(3):
+        slot_out(slot)
+    zeroth("d1")
+    decays()
+    second_ring_g()
     token_step(1)
     first_ring("d0")
-    first_ring("d1")
-    forward_weights()
+    slot_on(0)
+    gradient_states()
     sibling_first("g")
     hidden((1, 2, 1), (3, 1))
+    first_ring("d1")
+    slot_on(1)
+    slot_last(0)
+    forward_weights()
     token_step(2)
+    slot_sibling(0)
     hidden((1, 2, 1), (2, 1))
-    third("g")
+    slot_on(2)
+    slot_last(1)
+    hidden((0, 2, 1), (1, 1), 512)
+    third_g()
+    slot_sibling(1)
+    hidden((2, 2, 1), (1, 1), 512)
     token_step(3)
-    second_ring("d0")
-    second_ring("d1")
+    slot_on(3)
+    second_ring_a("d0")
+    slot_last(2)
     sibling_third("g")
-    hidden((3, 2, 2), (2, 2))
-    hidden((1, 2, 3), (1, 1))
+    hidden((3, 2, 2), (1, 1), 512)
     for buf, keys in ((xall, kx), (gall, kg)):
         arrived(keys["lo"], buf.at[SLOT[4], pl.ds(0, T // 2)])
         arrived(keys["hi"], buf.at[SLOT[4], pl.ds(T // 2, T // 2)])
-    fourth("g")
-    hidden((1, 2, 3), (0, 1))
-    sibling_last("g")
-    hidden((0, 2, 2), (0, 4))
+    slot_sibling(2)
+    hidden((0, 1, 2), (0, 1), 512)
+    slot_last(3)
+    fourth_g()
+    second_ring_b("d0")
+    hidden((2, 1, 4), (0, 1), 512)
     third("d0")
-    hidden((4, 2, 2), (0, 4))
-    hidden((7, 2, 1), (0, 4))
+    second_ring_a("d1")
+    second_ring_b("d1")
+    slot_sibling(3)
+    sibling_fourth_g()
+    hidden((4, 2, 1), (1, 1), 512)
+    hidden((6, 1, 1), (0, 2), 512)
+    fourth("d0")
+    hidden((7, 1, 1), (0, 2), 512)
     third("d1")
-    fourth("d0")
     sibling_first("d0")
     sibling_third("d0")
     sibling_last("d0")
@@ -589,11 +663,23 @@
     for stage in (forward_one, forward_two, forward_three, forward_four):
         stage(2)
         stage(3)
+    assert counter[0] == COPIES, counter
     for c in sent:
         c.wait_send()
 
 
-COPIES = 2 + 3 * 27 + 2 + 12 + 28 + 1 + 4 + 16
+COPIES = 2 + 2 * 27 + (5 + 6 + 16 + 4 + 3 + 3 + 4 + 2) + 2 + 12 + 28 + 1 + 4 + 16
+
+
+def hand_over(a_ref, b_ref, out_a, out_b, sems):
+    copies = [
+        pltpu.make_async_copy(a_ref, out_a, sems.at[0]),
+        pltpu.make_async_copy(b_ref, out_b, sems.at[1]),
+    ]
+    for c in copies:
+        c.start()
+    for c in copies:
+        c.wait()
 
 
 def on_device(
@@ -608,7 +694,7 @@
     state = pltpu.VMEM((N, D), BF16)
     half = pltpu.VMEM((N // 2, D), BF16)
     row = pltpu.VMEM((8, D), F32)
-    return pl.pallas_call(
+    out, grad = pl.pallas_call(
         kernel,
         out_shape=[jax.ShapeDtypeStruct((1, T, D), BF16)] * 2,
         in_specs=[hbm, vmem, hbm, hbm, hbm, hbm] + [vmem] * 8,
@@ -639,9 +725,16 @@
             collective_id=0, has_side_effects=True, vmem_limit_bytes=63 * 2**20
         ),
     )(
-        tokens, router, gate_up, down, shared_gate_up, shared_down, routes, lengths,
-        steps, writes, reads, decay_rate.reshape(1, -1), skip_gain.reshape(1, -1), cotangent,
+        tokens, router.T, gate_up, down, shared_gate_up, shared_down, jnp.swapaxes(routes, 1, 2), lengths,
+        jnp.swapaxes(steps, 1, 2), writes, reads, decay_rate.reshape(1, -1), skip_gain.reshape(1, -1), cotangent,
     )
+    return pl.pallas_call(
+        hand_over,
+        out_shape=[jax.ShapeDtypeStruct((1, T, D), BF16)] * 2,
+        in_specs=[hbm, hbm],
+        out_specs=[hbm, hbm],
+        scratch_shapes=[pltpu.SemaphoreType.DMA((2,))],
+    )(out, grad)
 
 
 def solution(mesh):

time: 185 us -> 226 us (1.22)
  Pallas kernels: 176 us -> 225 us
  local copies, waits for them, and re-layouts: 8.84 us -> 0 us
    pallas_call x0 -> x1, Pallas kernels: none -> 40.8 us  [on_device(): pl.pallas_call(hand_over, out_shape=[jax.ShapeDtypeStruct((1, T, D), BF16...]
    unnamed x5 -> x0, local copies, waits for them, and re-layouts: 8.84 us -> none
    pallas_call x1, Pallas kernels: 176 us -> 184 us  [on_device(): pl.pallas_call(kernel, out_shape=[jax.ShapeDtypeStruct((1, T, D), BF16)]...]
where the time goes in v3:
time: 226 us
  Pallas kernels  225 us (100%)
    pallas_call x1, Pallas kernels, on_device(): pl.pallas_call(kernel, out_shape=[jax.ShapeDtypeStruct((1, T, D), BF16)]...  184 us
    pallas_call x1, Pallas kernels, on_device(): pl.pallas_call(hand_over, out_shape=[jax.ShapeDtypeStruct((1, T, D), BF16...  40.8 us

profile of v3, /device:TPU:1, one launch (start us, length us, event | category | flops | bytes accessed | tf_op | source)
XLA Modules:
  0.0 226.1 jit_solution(7870644850701366779)
XLA Ops:
  0.6 184.4 %shard_map.149 = (bf16[1,128,2560]{2,1,0:T(8,128)(2,1)}, bf16[1,128,2560]{2,1,0:T(8,128)(2,1)}) custom-call(bf16[1,128,2560]{2,1,0:T(8,128)(2,1)} %x_hbm.1, bf16[64,2560]{1,0:T(8,128)(2,1)} %bitcast.5, bf16[2,320,512]{2,1,0:T(8,128)(2,1)} %gu_hbm.1, bf16[2,32,2560]{2,1,0:T(8,128)(2,1)} %dn_hbm.1, bf16[2560,512]{1,0:T(8,128)(2,1)} %sgu_hbm.1, ...), custom_call_target="tpu_custom_call" | custom-call | tf_op jit(solution)/shard_map/pallas_call | solution.py:697
  185.0 40.8 %shard_map.150 = (bf16[1,128,2560]{2,1,0:T(8,128)(2,1)}, bf16[1,128,2560]{2,1,0:T(8,128)(2,1)}) custom-call(bf16[1,128,2560]{2,1,0:T(8,128)(2,1)} %get-tuple-element.4.a_ref, bf16[1,128,2560]{2,1,0:T(8,128)(2,1)} %get-tuple-element.5.b_ref), custom_call_target="tpu_custom_call" | custom-call | tf_op jit(solution)/shard_map/pallas_call | solution.py:731

commit v4 on v3

--- a/solution.py
+++ b/solution.py
@@ -278,8 +278,8 @@
         arrived(key[name, "fA"], region(name, every, 0, y2, other))
         arrived(key[name, "fB"], region(name, 3, 1, every, other))
 
-    zeroth("g")
-    zeroth("d0")
+    for name in ("g", "d0", "d1"):
+        zeroth(name)
     lg = pltpu.make_async_copy(gu_hbm, wg.at[0, :, y, core], loc.at[1])
     ld = pltpu.make_async_copy(dn_hbm, wd.at[0, :, y, core], loc.at[2])
     lg.start()
@@ -571,60 +571,60 @@
     lg.wait()
     ld.wait()
     shared_expert()
+    decays()
     first_ring("g")
     for slot in range(3):
         slot_out(slot)
-    zeroth("d1")
-    decays()
+    first_ring("d0")
+    first_ring("d1")
+    token_step(1)
     second_ring_g()
-    token_step(1)
-    first_ring("d0")
-    slot_on(0)
     gradient_states()
+    forward_weights()
     sibling_first("g")
     hidden((1, 2, 1), (3, 1))
-    first_ring("d1")
+    slot_on(0)
     slot_on(1)
-    slot_last(0)
-    forward_weights()
     token_step(2)
-    slot_sibling(0)
     hidden((1, 2, 1), (2, 1))
     slot_on(2)
-    slot_last(1)
-    hidden((0, 2, 1), (1, 1), 512)
-    third_g()
-    slot_sibling(1)
-    hidden((2, 2, 1), (1, 1), 512)
     token_step(3)
     slot_on(3)
+    third_g()
     second_ring_a("d0")
-    slot_last(2)
+    second_ring_b("d0")
+    slot_last(0)
     sibling_third("g")
     hidden((3, 2, 2), (1, 1), 512)
+    slot_last(1)
+    slot_sibling(0)
+    hidden((0, 1, 1), (1, 1), 512)
     for buf, keys in ((xall, kx), (gall, kg)):
         arrived(keys["lo"], buf.at[SLOT[4], pl.ds(0, T // 2)])
         arrived(keys["hi"], buf.at[SLOT[4], pl.ds(T // 2, T // 2)])
-    slot_sibling(2)
-    hidden((0, 1, 2), (0, 1), 512)
+    slot_last(2)
+    hidden((1, 2, 2), (0, 1), 512)
+    slot_sibling(1)
+    hidden((2, 1, 1), (1, 1), 512)
     slot_last(3)
     fourth_g()
-    second_ring_b("d0")
-    hidden((2, 1, 4), (0, 1), 512)
+    hidden((5, 1, 1), (0, 1), 512)
+    hidden((0, 2, 2), (0, 1), 512)
+    slot_sibling(2)
+    hidden((4, 1, 1), (0, 2), 512)
     third("d0")
     second_ring_a("d1")
     second_ring_b("d1")
     slot_sibling(3)
-    sibling_fourth_g()
-    hidden((4, 2, 1), (1, 1), 512)
     hidden((6, 1, 1), (0, 2), 512)
     fourth("d0")
+    sibling_fourth_g()
     hidden((7, 1, 1), (0, 2), 512)
-    third("d1")
     sibling_first("d0")
     sibling_third("d0")
     sibling_last("d0")
     scatter_start(0)
+    third("d1")
     relay(0, 0)
     partial(SLOT[2], 2 * T, 0, part)
     fourth("d1")
@@ -671,15 +671,9 @@
 COPIES = 2 + 2 * 27 + (5 + 6 + 16 + 4 + 3 + 3 + 4 + 2) + 2 + 12 + 28 + 1 + 4 + 16
 
 
-def hand_over(a_ref, b_ref, out_a, out_b, sems):
-    copies = [
-        pltpu.make_async_copy(a_ref, out_a, sems.at[0]),
-        pltpu.make_async_copy(b_ref, out_b, sems.at[1]),
-    ]
-    for c in copies:
-        c.start()
-    for c in copies:
-        c.wait()
+def hand_over(a_ref, b_ref, out_a, out_b):
+    out_a[...] = a_ref[...]
+    out_b[...] = b_ref[...]
 
 
 def on_device(
@@ -731,9 +725,8 @@
     return pl.pallas_call(
         hand_over,
         out_shape=[jax.ShapeDtypeStruct((1, T, D), BF16)] * 2,
-        in_specs=[hbm, hbm],
-        out_specs=[hbm, hbm],
-        scratch_shapes=[pltpu.SemaphoreType.DMA((2,))],
+        in_specs=[vmem, vmem],
+        out_specs=[vmem, vmem],
     )(out, grad)
 
 

time: 226 us -> 170 us (0.75)
  Pallas kernels: 225 us -> 169 us
    pallas_call x1, Pallas kernels: 40.8 us -> 2.38 us  [on_device(): pl.pallas_call(hand_over, out_shape=[jax.ShapeDtypeStruct((1, T, D), BF16...]
    pallas_call x1, Pallas kernels: 184 us -> 167 us  [on_device(): pl.pallas_call(kernel, out_shape=[jax.ShapeDtypeStruct((1, T, D), BF16)]...]
where the time goes in v4:
time: 170 us
  Pallas kernels  169 us (99%)
    pallas_call x1, Pallas kernels, on_device(): pl.pallas_call(kernel, out_shape=[jax.ShapeDtypeStruct((1, T, D), BF16)]...  167 us

profile of v4, /device:TPU:1, one launch (start us, length us, event | category | flops | bytes accessed | tf_op | source)
XLA Modules:
  0.0 169.6 jit_solution(8728154711233351191)
XLA Ops:
  0.6 166.6 %shard_map.149 = (bf16[1,128,2560]{2,1,0:T(8,128)(2,1)}, bf16[1,128,2560]{2,1,0:T(8,128)(2,1)}) custom-call(bf16[1,128,2560]{2,1,0:T(8,128)(2,1)} %x_hbm.1, bf16[64,2560]{1,0:T(8,128)(2,1)} %bitcast.5, bf16[2,320,512]{2,1,0:T(8,128)(2,1)} %gu_hbm.1, bf16[2,32,2560]{2,1,0:T(8,128)(2,1)} %dn_hbm.1, bf16[2560,512]{1,0:T(8,128)(2,1)} %sgu_hbm.1, ...), custom_call_target="tpu_custom_call" | custom-call | tf_op jit(solution)/shard_map/pallas_call | solution.py:691
  167.2 2.4 %shard_map.150 = (bf16[1,128,2560]{2,1,0:T(8,128)(2,1)}, bf16[1,128,2560]{2,1,0:T(8,128)(2,1)}) custom-call(bf16[1,128,2560]{2,1,0:T(8,128)(2,1)} %get-tuple-element.4.a_ref, bf16[1,128,2560]{2,1,0:T(8,128)(2,1)} %get-tuple-element.5.b_ref), custom_call_target="tpu_custom_call" | custom-call | tf_op jit(solution)/shard_map/pallas_call | solution.py:725

commit v5 on v4

--- a/solution.py
+++ b/solution.py
@@ -472,6 +472,8 @@
         v = (closing[:, cols] * u.astype(F32)).astype(BF16)
         lown[:, cols] = jnp.dot(bt[...], v, preferred_element_type=F32).astype(BF16)
         key["l", q] = send(lown.at[:, cols], lsib.at[:, cols], sib)
+
+    def forward_inside(q, u):
         left = col_i < 64
         for i in range(Q // N):
             p = q * (Q // N) + i
@@ -562,11 +564,15 @@
         for k in (5, 6):
             arrived(kr[hf, k], rr.at[hf, k])
             arrived(kl[hf, k], rl.at[hf, k])
+        us = []
         for i, (a, b) in enumerate(((6, 5), (5, 6))):
             q = 2 * hf + i
             cols = slice(q * Q, (q + 1) * Q)
             u = shared[:, cols] + rr[hf, a].astype(F32) + rl[hf, b].astype(F32)
-            forward_zero(q, u.astype(BF16))
+            us.append(u.astype(BF16))
+            forward_zero(q, us[-1])
+        for i, u in enumerate(us):
+            forward_inside(2 * hf + i, u)
 
     lg.wait()
     ld.wait()
@@ -606,10 +612,10 @@
     hidden((1, 2, 2), (0, 1), 512)
     slot_sibling(1)
     hidden((2, 1, 1), (1, 1), 512)
+    hidden((5, 1, 1), (0, 1), 512)
+    hidden((0, 2, 2), (0, 1), 512)
     slot_last(3)
     fourth_g()
-    hidden((5, 1, 1), (0, 1), 512)
-    hidden((0, 2, 2), (0, 1), 512)
     slot_sibling(2)
     hidden((4, 1, 1), (0, 2), 512)
     third("d0")

time: 170 us -> 170 us (level)
  no operation moved by 1% of the time
where the time goes in v5:
time: 170 us
  Pallas kernels  169 us (99%)
    pallas_call x1, Pallas kernels, on_device(): pl.pallas_call(kernel, out_shape=[jax.ShapeDtypeStruct((1, T, D), BF16)]...  167 us

profile of v5, /device:TPU:1, one launch (start us, length us, event | category | flops | bytes accessed | tf_op | source)
XLA Modules:
  0.0 170.0 jit_solution(5473049918407240511)
XLA Ops:
  0.6 166.9 %shard_map.149 = (bf16[1,128,2560]{2,1,0:T(8,128)(2,1)}, bf16[1,128,2560]{2,1,0:T(8,128)(2,1)}) custom-call(bf16[1,128,2560]{2,1,0:T(8,128)(2,1)} %x_hbm.1, bf16[64,2560]{1,0:T(8,128)(2,1)} %bitcast.5, bf16[2,320,512]{2,1,0:T(8,128)(2,1)} %gu_hbm.1, bf16[2,32,2560]{2,1,0:T(8,128)(2,1)} %dn_hbm.1, bf16[2560,512]{1,0:T(8,128)(2,1)} %sgu_hbm.1, ...), custom_call_target="tpu_custom_call" | custom-call | tf_op jit(solution)/shard_map/pallas_call | solution.py:697
  167.6 2.4 %shard_map.150 = (bf16[1,128,2560]{2,1,0:T(8,128)(2,1)}, bf16[1,128,2560]{2,1,0:T(8,128)(2,1)}) custom-call(bf16[1,128,2560]{2,1,0:T(8,128)(2,1)} %get-tuple-element.4.a_ref, bf16[1,128,2560]{2,1,0:T(8,128)(2,1)} %get-tuple-element.5.b_ref), custom_call_target="tpu_custom_call" | custom-call | tf_op jit(solution)/shard_map/pallas_call | solution.py:731
